TPU v7x, 32 devices: a whole 2x2x4 slice. The times are simulated.
32 devices in a mesh: exp: 8 (over y, x, core), seq: 4 (over z).
Axes of the slice: x: 2, y: 2, z: 4, core: 2. Of those that a mesh axis runs over, the one named last changes fastest.
Arguments:
- queries: bfloat16 [4096, 2048], P(('exp', 'seq')), may hold values from -400 to 400
- keys: bfloat16 [4096, 256], P(('exp', 'seq')), may hold values from -5 to 5
- values: bfloat16 [4096, 256], P(('exp', 'seq')), may hold values from -6 to 6
- resid: bfloat16 [4096, 2048], P(('exp', 'seq')), may hold values from -50 to 50
- seg_ids: int32 [4096], P('exp'), may hold values from 0 to 63, never falling along the last dimension, each value on 1 to 256 neighbouring positions
- norm_gain: float32 [2048], replicated, may hold values from 0.1 to 1.9
- expert_ids: int32 [4096], P(('exp', 'seq')), may hold values from 0 to 31, as said below
- gate_weights: float32 [4096], P(('exp', 'seq')), may hold values from 0.1 to 0.9
- w_in: bfloat16 [32, 2048, 1536], P(('exp', 'seq')), may hold values from -0.125 to 0.125
- w_out: bfloat16 [32, 768, 2048], P(('exp', 'seq')), may hold values from -0.21875 to 0.21875
Outputs:
- output: bfloat16 [4096, 2048], P(('exp', 'seq'))
Inputs may be any that keep to these rules, and one draw needn't show every extreme that they name: `expert_ids`: within each aligned block of 128 tokens (the tokens of one device) no expert is named more than 8 times, and the bound is reached.
All inputs are finite; a program needn't handle non-finite values.
Results may differ from a plain program's by a relative error of at most 0.0055.
Values may be sent and summed in bfloat16 or wider, within the bound.
No kernel may reach another device: no remote copies, remote signals or barrier semaphores. Data moves between devices by JAX's collectives and lax.ppermute only.
A program may use at most 64 MiB of HBM per device.

v0:
```python
import math

import jax
import jax.numpy as jnp
from jax import lax
from jax.sharding import PartitionSpec as P

HD = 128
HEADS = 16
KVH = 2
EXP_DEV = 4


def expert_parts(rows_in, stack_in, stack_out):
    group_units = stack_out.shape[1]
    gate_up = jnp.einsum("rd,qdf->qrf", rows_in, stack_in, preferred_element_type=jnp.float32)
    active = (jax.nn.silu(gate_up[..., :group_units]) * gate_up[..., group_units:]).astype(
        jnp.bfloat16
    )
    return jnp.einsum("qrf,qfd->qrd", active, stack_out, preferred_element_type=jnp.float32).astype(
        jnp.bfloat16
    )


def per_device(
    queries, keys, values, resid, seg_ids, norm_gain, expert_ids, gate_weights, w_in, w_out
):
    seq_count = lax.axis_size("seq")
    exp_count = lax.axis_size("exp")
    tok_rows = queries.shape[0]
    length = tok_rows * seq_count
    model_width = resid.shape[1]
    local_heads = HEADS // seq_count
    head_group = HEADS // KVH
    splits = seq_count // EXP_DEV
    position = jnp.arange(length)
    scale_by = 1.0 / math.sqrt(HD)
    local_queries = lax.all_to_all(queries, "seq", split_axis=1, concat_axis=0, tiled=True)
    gathered_keys, gathered_values = (
        lax.all_gather(keys, "seq", axis=0, tiled=True),
        lax.all_gather(values, "seq", axis=0, tiled=True),
    )
    wanted = (lax.axis_index("seq") * local_heads + jnp.arange(local_heads)) // head_group
    local_keys = jnp.take(gathered_keys.reshape(length, KVH, HD), wanted, axis=1)
    local_values = jnp.take(gathered_values.reshape(length, KVH, HD), wanted, axis=1)
    local_queries = local_queries.reshape(length, local_heads, HD)
    block_rows = min(512, length)
    outputs = []
    for block_index in range(length // block_rows):
        low_row = block_index * block_rows
        high_row = low_row + block_rows
        scores = (
            jnp.einsum(
                "qhd,khd->hqk",
                local_queries[low_row:high_row],
                local_keys[:high_row],
                preferred_element_type=jnp.float32,
            )
            * scale_by
        )
        allowed = (seg_ids[low_row:high_row, None] == seg_ids[None, :high_row]) & (
            position[None, :high_row] <= position[low_row:high_row, None]
        )
        masked = jnp.where(allowed[None], scores, -jnp.inf)
        rowmax = jnp.max(masked, axis=-1, keepdims=True)
        weights = jnp.where(allowed[None], jnp.exp(scores - rowmax), 0.0)
        totals = jnp.sum(weights, axis=-1)
        mixture = jnp.einsum(
            "hqk,khd->qhd",
            weights.astype(jnp.bfloat16),
            local_values[:high_row],
            preferred_element_type=jnp.float32,
        )
        mixture = mixture / jnp.transpose(totals)[:, :, None]
        outputs.append(mixture.astype(jnp.bfloat16).reshape(block_rows, local_heads * HD))
    attended_heads = jnp.concatenate(outputs, 0)
    attended = lax.all_to_all(attended_heads, "seq", split_axis=0, concat_axis=1, tiled=True)
    hidden = (resid.astype(jnp.float32) + attended.astype(jnp.float32)).astype(jnp.bfloat16)
    hidden_float = hidden.astype(jnp.float32)
    meansq = jnp.mean(hidden_float * hidden_float, axis=-1, keepdims=True)
    normed = (hidden_float * lax.rsqrt(meansq + 1e-06) * norm_gain).astype(jnp.bfloat16)
    experts = EXP_DEV * exp_count
    capacity = max(2, 2 * tok_rows // experts)
    onehot = (expert_ids[:, None] == jnp.arange(experts)[None, :]).astype(jnp.int32)
    rank_in = jnp.sum(jnp.cumsum(onehot, axis=0) * onehot, axis=1) - 1
    slot_of = expert_ids * capacity + rank_in
    placing = (slot_of[None, :] == jnp.arange(experts * capacity)[:, None]).astype(jnp.bfloat16)
    outgoing = jnp.dot(placing, normed, preferred_element_type=jnp.float32).astype(jnp.bfloat16)
    outgoing = outgoing.reshape(exp_count, EXP_DEV * capacity, model_width)
    arrived = lax.all_to_all(outgoing, "exp", split_axis=0, concat_axis=0, tiled=True).reshape(
        exp_count, EXP_DEV, capacity, model_width
    )
    copies = jnp.repeat(jnp.transpose(arrived, (1, 0, 2, 3)), splits, axis=0)
    batch_rows = lax.all_to_all(copies, "seq", split_axis=0, concat_axis=0, tiled=True)
    partial_value = expert_parts(batch_rows.reshape(-1, model_width), w_in, w_out)[0].reshape(
        batch_rows.shape
    )
    returned = lax.all_to_all(partial_value, "seq", split_axis=0, concat_axis=0, tiled=True)
    summed = jnp.sum(
        returned.reshape(EXP_DEV, splits, exp_count, capacity, model_width),
        axis=1,
        dtype=jnp.float32,
    ).astype(jnp.bfloat16)
    results = jnp.transpose(summed, (1, 0, 2, 3))
    delivered = lax.all_to_all(
        results.reshape(exp_count, EXP_DEV * capacity, model_width),
        "exp",
        split_axis=0,
        concat_axis=0,
        tiled=True,
    )
    picking = (slot_of[:, None] == jnp.arange(experts * capacity)[None, :]).astype(jnp.bfloat16)
    routed = jnp.dot(
        picking, delivered.reshape(-1, model_width), preferred_element_type=jnp.float32
    )
    return (hidden_float + gate_weights[:, None] * routed).astype(jnp.bfloat16)


def solution(mesh):
    placed = (
        P(("exp", "seq"), None),
        P(("exp", "seq"), None),
        P(("exp", "seq"), None),
        P(("exp", "seq"), None),
        P("exp"),
        P(),
        P(("exp", "seq")),
        P(("exp", "seq")),
        P(("exp", "seq"), None, None),
        P(("exp", "seq"), None, None),
    )
    return jax.shard_map(
        per_device, mesh=mesh, in_specs=placed, out_specs=P(("exp", "seq"), None), check_vma=False
    )
```

profile of v0, /device:TPU:1, one launch (start us, length us, event | category | flops | bytes accessed | tf_op | source)
XLA Modules:
  0.0 182.4 jit_solution(14205509013194704203)
XLA Ops:
  0.0 2.0 %copy.51 = bf16[16,4,8,512]{3,2,0,1:T(8,128)(2,1)} copy(bf16[16,4,8,512]{3,2,1,0:T(8,128)(2,1)} %bitcast.83) | data formatting | bytes 1048576 | tf_op jit(solution)/shard_map/all_to_all | solution.py:38
  2.0 5.4 %all-to-all-start = ((bf16[128,4,512]{2,0,1:T(8,128)(2,1)}), bf16[128,4,512]{2,0,1:T(8,128)(2,1)}, u32[]{:S(2)}, u32[]{:S(2)}) async-start(bf16[128,4,512]{2,0,1:T(8,128)(2,1)} %bitcast.78), calls=%async_computation | async-start | bytes 1048576 | tf_op jit(solution)/shard_map/all_to_all | solution.py:38
  8.4 18.2 %all_gather.7 = bf16[512,256]{0,1:T(8,128)(2,1)} all-gather(bf16[128,256]{0,1:T(8,128)(2,1)S(1)} %copy.32), channel_id=1, replica_groups=mesh['exp'=8,'seq'=4] {'seq'}, dimensions={0}, use_global_device_ids=true | all-gather | bytes 327680 | tf_op jit(solution)/shard_map/all_gather | solution.py:40
  28.7 10.8 %all_gather.6 = bf16[512,256]{0,1:T(8,128)(2,1)} all-gather(bf16[128,256]{0,1:T(8,128)(2,1)S(1)} %copy.30), channel_id=1, replica_groups=mesh['exp'=8,'seq'=4] {'seq'}, dimensions={0}, use_global_device_ids=true | all-gather | bytes 327680 | tf_op jit(solution)/shard_map/all_gather | solution.py:41
  39.5 1.8 copy.31
  41.4 1.4 gather_fusion.1
  42.8 2.4 %gather_fusion = bf16[4,512,128]{2,1,0:T(8,128)(2,1)} fusion(bf16[512,2,128]{2,0,1:T(8,128)(2,1)} %copy.31, s32[1024]{0:T(1024)S(1)} %pad_clamp_fusion), kind=kCustom, calls=%fused_computation.clone | custom fusion | bytes 1048592 | tf_op jit(solution)/shard_map/jit(_take)/gather | solution.py:45
  45.4 2.0 %reshape.114 = bf16[512,4,128]{2,1,0:T(4,128)(2,1)} reshape(bf16[4,128,512]{2,1,0:T(8,128)(2,1)} %bitcast.4) | data formatting | bytes 1048576 | tf_op jit(solution)/shard_map/reshape | solution.py:46
  47.4 1.9 %fusion.37 = f32[4,512,512]{2,1,0:T(8,128)S(1)} fusion(bf16[512,4,128]{2,1,0:T(4,128)(2,1)} %reshape.114, bf16[4,512,128]{2,1,0:T(8,128)(2,1)} %gather_fusion.1, pred[4]{0:T(512)(128)(4,1)S(1)} %compare_and_fusion), kind=kOutput, calls=%fused_computation.39 | convolution fusion | flops 268697600 | bytes 5242884 | tf_op jit(solution)/shard_map/qhd,khd->hqk/dot_general | solution.py:53
  49.3 2.1 %fusion.59 = (f32[4,512]{1,0:T(4,128)S(1)}, bf16[4,512,512]{1,2,0:T(8,128)(2,1)S(1)}) fusion(f32[4,512,512]{2,1,0:T(8,128)S(1)} %fusion.37, pred[512,512]{0,1:T(8,128)(4,1)S(1)} %fusion.34), kind=kOutput, calls=%fused_computation.73 | output fusion | flops 7340543 | bytes 6561792 | tf_op jit(solution)/shard_map/sub | solution.py:66
  51.4 1.4 fusion.28
  52.9 2.0 %all_to_all.37 = bf16[4,128,512]{1,0,2:T(4,128)(2,1)} reshape(bf16[512,4,128]{0,2,1:T(8,128)(2,1)} %fusion.28) | data formatting | bytes 1048576 | tf_op jit(solution)/shard_map/all_to_all | solution.py:77
  54.8 1.9 %copy.38 = bf16[4,128,512]{1,2,0:T(8,128)(2,1)} copy(bf16[4,128,512]{1,0,2:T(4,128)(2,1)} %all_to_all.37) | data formatting | bytes 1048576 | tf_op jit(solution)/shard_map/all_to_all | solution.py:77
  56.7 4.1 %all-to-all-start.1 = ((bf16[4,128,512]{1,2,0:T(8,128)(2,1)}), bf16[4,128,512]{1,2,0:T(8,128)(2,1)}, u32[]{:S(2)}, u32[]{:S(2)}) async-start(bf16[4,128,512]{1,2,0:T(8,128)(2,1)} %copy.38), calls=%async_computation.1 | async-start | bytes 1048576 | tf_op jit(solution)/shard_map/all_to_all | solution.py:77
  61.3 8.7 %all-to-all-done.1 = bf16[4,128,512]{1,2,0:T(8,128)(2,1)} async-done(((bf16[4,128,512]{1,2,0:T(8,128)(2,1)}), bf16[4,128,512]{1,2,0:T(8,128)(2,1)}, u32[]{:S(2)}, u32[]{:S(2)}) %all-to-all-start.1) | async-done | bytes 524320 | tf_op jit(solution)/shard_map/all_to_all | solution.py:77
  70.1 2.1 %convert_element_type.63 = f32[4,128,512]{1,2,0:T(8,128)} convert(bf16[4,128,512]{1,2,0:T(8,128)(2,1)} %all-to-all-done.1) | non-fusion elementwise | flops 262144 | bytes 1572864 | tf_op jit(solution)/shard_map/convert_element_type | solution.py:78
  72.2 2.6 %copy.44 = f32[128,2048]{1,0:T(8,128)} copy(f32[128,2048]{0,1:T(8,128)} %bitcast.73) | data formatting | bytes 2097152 | tf_op jit(solution)/shard_map/convert_element_type | solution.py:78
  74.8 1.6 fusion.31
  76.9 25.2 %all_to_all.49 = bf16[8,32,2048]{2,1,0:T(8,128)(2,1)S(1)} all-to-all(bf16[8,32,2048]{2,1,0:T(8,128)(2,1)S(1)} %bitcast.74), channel_id=1, replica_groups=mesh['exp'=8,'seq'=4] {'exp'}, dimensions={0} | all-to-all | bytes 2097152 | tf_op jit(solution)/shard_map/all_to_all | solution.py:90
  102.2 27.2 %all_to_all.50 = bf16[4,8,8,2048]{3,2,1,0:T(8,128)(2,1)S(1)} all-to-all(bf16[4,8,8,2048]{3,2,1,0:T(8,128)(2,1)S(1)} %copy.40), channel_id=1, replica_groups=mesh['exp'=8,'seq'=4] {'seq'}, dimensions={0} | all-to-all | bytes 2097152 | tf_op jit(solution)/shard_map/all_to_all | solution.py:94
  129.4 4.6 %fusion.9 = f32[1,256,1536]{2,1,0:T(8,128)S(1)} fusion(bf16[256,2048]{1,0:T(8,128)(2,1)S(1)} %bitcast.81, bf16[1,2048,1536]{2,1,0:T(8,128)(2,1)} %param.20), kind=kOutput, calls=%fused_computation.13 | convolution fusion | flops 1610612736 | bytes 8912896 | tf_op jit(solution)/shard_map/rd,qdf->qrf/dot_general | solution.py:16
  135.1 27.8 %all_to_all.51 = bf16[4,8,8,2048]{3,2,1,0:T(8,128)(2,1)S(1)} all-to-all(bf16[4,8,8,2048]{3,2,1,0:T(8,128)(2,1)S(1)} %bitcast.82), channel_id=1, replica_groups=mesh['exp'=8,'seq'=4] {'seq'}, dimensions={0} | all-to-all | bytes 2097152 | tf_op jit(solution)/shard_map/all_to_all | solution.py:98
  162.9 18.4 %all_to_all.52 = bf16[8,32,2048]{2,1,0:T(8,128)(2,1)S(1)} all-to-all(bf16[8,32,2048]{2,1,0:T(8,128)(2,1)S(1)} %bitcast.76), channel_id=1, replica_groups=mesh['exp'=8,'seq'=4] {'exp'}, dimensions={0} | all-to-all | bytes 2097152 | tf_op jit(solution)/shard_map/all_to_all | solution.py:105
  181.3 1.1 fusion.16
  (29 shorter events, 5.5 us)
Async XLA Ops:
  0.0 134.0 %copy-start = (bf16[1,768,2048]{2,1,0:T(8,128)(2,1)S(1)}, bf16[1,768,2048]{2,1,0:T(8,128)(2,1)}, u32[]{:S(2)}) copy-start(bf16[1,768,2048]{2,1,0:T(8,128)(2,1)} %param.21) | copy-start | bytes 9437188
  0.0 45.2 %copy-start.3 = (s32[512]{0:T(512)S(1)}, s32[512]{0:T(512)}, u32[]{:S(2)}) copy-start(s32[512]{0:T(512)} %param.16) | copy-start | bytes 6148
  2.0 43.3 %all-to-all-start = ((bf16[128,4,512]{2,0,1:T(8,128)(2,1)}), bf16[128,4,512]{2,0,1:T(8,128)(2,1)}, u32[]{:S(2)}, u32[]{:S(2)}) async-start(bf16[128,4,512]{2,0,1:T(8,128)(2,1)} %bitcast.78), calls=%async_computation | async-start | bytes 1048576 | tf_op jit(solution)/shard_map/all_to_all | solution.py:38
  49.3 2.1 %copy-start.1 = (bf16[4,512,128]{2,1,0:T(8,128)(2,1)S(1)}, bf16[4,512,128]{2,1,0:T(8,128)(2,1)}, u32[]{:S(2)}) copy-start(bf16[4,512,128]{2,1,0:T(8,128)(2,1)} %gather_fusion) | copy-start | bytes 1572868
  51.4 9.5 %copy-start.4 = (s32[128]{0:T(128)S(1)}, s32[128]{0:T(128)}, u32[]{:S(2)}) copy-start(s32[128]{0:T(128)} %param.18) | copy-start | bytes 1540
  54.8 21.6 %copy-start.2 = (f32[2048]{0:T(1024)S(1)}, f32[2048]{0:T(1024)}, u32[]{:S(2)}) copy-start(f32[2048]{0:T(1024)} %param.17) | copy-start | bytes 24580
  56.7 13.3 %all-to-all-start.1 = ((bf16[4,128,512]{1,2,0:T(8,128)(2,1)}), bf16[4,128,512]{1,2,0:T(8,128)(2,1)}, u32[]{:S(2)}, u32[]{:S(2)}) async-start(bf16[4,128,512]{1,2,0:T(8,128)(2,1)} %copy.38), calls=%async_computation.1 | async-start | bytes 1048576 | tf_op jit(solution)/shard_map/all_to_all | solution.py:77
  135.0 46.2 %copy-start.5 = (f32[128]{0:T(128)S(1)}, f32[128]{0:T(128)}, u32[]{:S(2)}) copy-start(f32[128]{0:T(128)} %param.19) | copy-start | bytes 1540
where the time goes:
time: 185 us; the launch traced here: 182 us
  blocking collectives  128 us (69%)
  local copies, waits for them, and re-layouts  19.3 us (10%)
  matrix products  10.6 us (6%)
  starting transfers between devices  9.56 us (5%)
  waiting for transfers between devices  8.74 us (5%)
  other arithmetic  6.47 us (3%)
    all_to_all x1, blocking collectives, per_device(): lax.all_to_all(partial_value, 'seq', split_axis=0, concat_axis=0, tiled=T...  27.8 us
    all_to_all x1, blocking collectives, per_device(): lax.all_to_all(copies, 'seq', split_axis=0, concat_axis=0, tiled=True)  27.2 us
    all_to_all x1, blocking collectives, per_device(): lax.all_to_all(outgoing, 'exp', split_axis=0, concat_axis=0, tiled=True)  25.2 us
    all_to_all x1, blocking collectives, per_device(): lax.all_to_all(results.reshape(exp_count, EXP_DEV * capacity, model_width...  18.4 us
    all_gather x1, blocking collectives, per_device(): lax.all_gather(keys, 'seq', axis=0, tiled=True)  18.2 us
    all_gather x1, blocking collectives, per_device(): lax.all_gather(values, 'seq', axis=0, tiled=True)  10.8 us
    all_to_all x1, waiting for transfers between devices, per_device(): lax.all_to_all(attended_heads, 'seq', split_axis=0, concat_axis=1, tiled=...  8.74 us
    all_to_all x1, starting transfers between devices, per_device(): lax.all_to_all(queries, 'seq', split_axis=1, concat_axis=0, tiled=True)  5.42 us
  transfers between devices with their start and end apart: 2, of which 1 were waited for; matrix products, arithmetic and copies ran while one was open for 5% of the time, Pallas kernels for 0%

commit v1 on v0

v1 whole, which is shorter than its diff:
```python
import functools
import math

import jax
import jax.numpy as jnp
from jax import lax
from jax.experimental import pallas as pl
from jax.experimental.pallas import tpu as pltpu
from jax.sharding import PartitionSpec as P

HD = 128
HEADS = 16
KVH = 2
EXP_DEV = 4
FF = 768
EPS = 1e-6
F32 = jnp.float32
BF16 = jnp.bfloat16
VMEM = pl.BlockSpec(memory_space=pltpu.VMEM)


def attend_kernel(
    blocks, splits, capacity, q_ref, *refs
):
    kv_refs = refs[:blocks]
    seg_q_ref, seg_k_ref, resid_ref, gain_ref, ids_col_ref, ids_row_ref = refs[blocks : blocks + 6]
    hidden_ref, outgoing_ref = refs[blocks + 6 :]
    rows = q_ref.shape[0]
    width = blocks * rows
    group = HEADS // KVH
    scale_by = 1.0 / math.sqrt(HD)
    key_at = lax.broadcasted_iota(jnp.int32, (rows, width), 1) - (width - rows)
    query_at = lax.broadcasted_iota(jnp.int32, (rows, width), 0)
    allowed = (seg_q_ref[...] == seg_k_ref[...]) & (key_at <= query_at)
    sumsq = jnp.zeros((rows, 1), F32)
    for kv_head in range(KVH):
        key_cols = slice(kv_head * HD, (kv_head + 1) * HD)
        value_cols = slice((KVH + kv_head) * HD, (KVH + kv_head + 1) * HD)
        head_keys = jnp.concatenate([ref[:, key_cols] for ref in kv_refs], 0)
        head_values = jnp.concatenate([ref[:, value_cols] for ref in kv_refs], 0)
        for head in range(kv_head * group, (kv_head + 1) * group):
            cols = slice(head * HD, (head + 1) * HD)
            scores = lax.dot_general(
                q_ref[:, cols], head_keys, (((1,), (1,)), ((), ())), preferred_element_type=F32
            )
            scores = jnp.where(allowed, scores * scale_by, -jnp.inf)
            weights = jnp.exp(scores - jnp.max(scores, axis=-1, keepdims=True))
            totals = jnp.sum(weights, axis=-1, keepdims=True)
            mixture = jnp.dot(weights.astype(BF16), head_values, preferred_element_type=F32)
            attended = (mixture / totals).astype(BF16).astype(F32)
            hidden = (resid_ref[:, cols].astype(F32) + attended).astype(BF16)
            hidden_ref[:, cols] = hidden
            hidden_float = hidden.astype(F32)
            sumsq += jnp.sum(hidden_float * hidden_float, axis=-1, keepdims=True)
    inverse = lax.rsqrt(sumsq / (HEADS * HD) + EPS)
    earlier = lax.broadcasted_iota(jnp.int32, (rows, rows), 0) < lax.broadcasted_iota(
        jnp.int32, (rows, rows), 1
    )
    same = (ids_col_ref[...] == ids_row_ref[...]) & earlier
    rank = jnp.sum(same.astype(F32), axis=0, keepdims=True).astype(jnp.int32)
    slots = outgoing_ref.shape[0]
    slot_at = lax.broadcasted_iota(jnp.int32, (slots, rows), 0)
    first = ids_row_ref[...] * (splits * capacity) + rank
    placing = slot_at == first
    for split in range(1, splits):
        placing = placing | (slot_at == first + split * capacity)
    placing = placing.astype(F32).astype(BF16)
    step = 512
    for low in range(0, HEADS * HD, step):
        cols = slice(low, low + step)
        normed = (hidden_ref[:, cols].astype(F32) * inverse * gain_ref[:, cols]).astype(BF16)
        outgoing_ref[:, cols] = jnp.dot(placing, normed, preferred_element_type=F32).astype(BF16)


def attend(splits, capacity, slots, queries, kv_blocks, seg_q, seg_k, resid, gain, ids):
    rows, model_width = resid.shape
    blocks = len(kv_blocks)
    return pl.pallas_call(
        functools.partial(attend_kernel, blocks, splits, capacity),
        out_shape=(
            jax.ShapeDtypeStruct((rows, model_width), BF16),
            jax.ShapeDtypeStruct((slots, model_width), BF16),
        ),
        in_specs=[VMEM] * (blocks + 7),
        out_specs=(VMEM, VMEM),
        compiler_params=pltpu.CompilerParams(vmem_limit_bytes=32 * 2**20),
        name="attend",
    )(queries, *kv_blocks, seg_q, seg_k, resid, gain, ids[:, None], ids[None, :])


def expert_kernel(x_ref, gate_ref, up_ref, down_ref, out_ref, total):
    step = pl.program_id(0)
    rows_in = x_ref[...]
    gate = jnp.dot(rows_in, gate_ref[0], preferred_element_type=F32)
    up = jnp.dot(rows_in, up_ref[0], preferred_element_type=F32)
    active = (gate / (1.0 + jnp.exp(-gate)) * up).astype(BF16)
    part = jnp.dot(active, down_ref[0], preferred_element_type=F32)

    @pl.when(step == 0)
    def _():
        total[...] = part

    @pl.when(step > 0)
    def _():
        total[...] += part

    @pl.when(step == pl.num_programs(0) - 1)
    def _():
        out_ref[...] = total[...].astype(BF16)


def experts(rows_in, w_in, w_out):
    rows, model_width = rows_in.shape
    units = w_out.shape[1]
    tile = 256
    if units % tile:
        gate_up = jnp.dot(rows_in, w_in[0], preferred_element_type=F32)
        active = (jax.nn.silu(gate_up[:, :units]) * gate_up[:, units:]).astype(BF16)
        return jnp.dot(active, w_out[0], preferred_element_type=F32).astype(BF16)
    steps = units // tile
    return pl.pallas_call(
        expert_kernel,
        grid=(steps,),
        out_shape=jax.ShapeDtypeStruct((rows, model_width), BF16),
        in_specs=[
            pl.BlockSpec((rows, model_width), lambda i: (0, 0)),
            pl.BlockSpec((1, model_width, tile), lambda i: (0, 0, i)),
            pl.BlockSpec((1, model_width, tile), lambda i: (0, 0, steps + i)),
            pl.BlockSpec((1, tile, model_width), lambda i: (0, i, 0)),
        ],
        out_specs=pl.BlockSpec((rows, model_width), lambda i: (0, 0)),
        scratch_shapes=[pltpu.VMEM((rows, model_width), F32)],
        compiler_params=pltpu.CompilerParams(vmem_limit_bytes=40 * 2**20),
        name="experts",
    )(rows_in, w_in, w_in, w_out)


def combine_kernel(splits, capacity, delivered_ref, hidden_ref, gate_ref, ids_col_ref, ids_row_ref, out_ref):
    rows = hidden_ref.shape[0]
    slots = delivered_ref.shape[0]
    earlier = lax.broadcasted_iota(jnp.int32, (rows, rows), 1) < lax.broadcasted_iota(
        jnp.int32, (rows, rows), 0
    )
    same = (ids_col_ref[...] == ids_row_ref[...]) & earlier
    rank = jnp.sum(same.astype(F32), axis=1, keepdims=True).astype(jnp.int32)
    first = ids_col_ref[...] * (splits * capacity) + rank
    slot_at = lax.broadcasted_iota(jnp.int32, (rows, slots), 1)
    picking = slot_at == first
    for split in range(1, splits):
        picking = picking | (slot_at == first + split * capacity)
    picking = picking.astype(F32).astype(BF16)
    step = 512
    for low in range(0, hidden_ref.shape[1], step):
        cols = slice(low, low + step)
        routed = jnp.dot(picking, delivered_ref[:, cols], preferred_element_type=F32)
        routed = routed.astype(BF16).astype(F32)
        out_ref[:, cols] = (hidden_ref[:, cols].astype(F32) + gate_ref[...] * routed).astype(BF16)


def combine(splits, capacity, delivered, hidden, gates, ids):
    return pl.pallas_call(
        functools.partial(combine_kernel, splits, capacity),
        out_shape=jax.ShapeDtypeStruct(hidden.shape, BF16),
        in_specs=[VMEM] * 5,
        out_specs=VMEM,
        compiler_params=pltpu.CompilerParams(vmem_limit_bytes=32 * 2**20),
        name="combine",
    )(delivered, hidden, gates[:, None], ids[:, None], ids[None, :])


def per_device(
    queries, keys, values, resid, seg_ids, norm_gain, expert_ids, gate_weights, w_in, w_out
):
    seq_count = lax.axis_size("seq")
    exp_count = lax.axis_size("exp")
    devices = seq_count * exp_count
    rows, model_width = resid.shape
    length = rows * seq_count
    splits = FF // w_out.shape[1]
    capacity = max(2, 2 * rows * splits // devices)
    slots = devices * capacity
    reach = length // 2
    before = min(seq_count - 1, -(-(reach - 1) // rows))
    place = lax.axis_index("seq")

    own = jnp.concatenate([keys, values], axis=1)
    kv_blocks = [
        lax.ppermute(own, "seq", [(i, i + hop) for i in range(seq_count - hop)])
        for hop in range(before, 0, -1)
    ] + [own]
    padded = jnp.concatenate([jnp.full((before * rows,), -1, jnp.int32), seg_ids])
    window = lax.dynamic_slice(padded, (place * rows,), ((before + 1) * rows,))
    seg_q, seg_k = window[before * rows :, None], window[None, :]
    hidden, outgoing = attend(
        splits, capacity, slots, queries, kv_blocks, seg_q, seg_k, resid, norm_gain[None, :], expert_ids
    )

    def exchange(block):
        return lax.all_to_all(
            block.reshape(devices, capacity, model_width),
            ("exp", "seq"),
            split_axis=0,
            concat_axis=0,
            tiled=True,
        ).reshape(slots, model_width)

    delivered = exchange(experts(exchange(outgoing), w_in, w_out))
    return combine(splits, capacity, delivered, hidden, gate_weights, expert_ids)


def solution(mesh):
    placed = (
        P(("exp", "seq"), None),
        P(("exp", "seq"), None),
        P(("exp", "seq"), None),
        P(("exp", "seq"), None),
        P("exp"),
        P(),
        P(("exp", "seq")),
        P(("exp", "seq")),
        P(("exp", "seq"), None, None),
        P(("exp", "seq"), None, None),
    )
    return jax.shard_map(
        per_device, mesh=mesh, in_specs=placed, out_specs=P(("exp", "seq"), None), check_vma=False
    )
```

time: 185 us -> 97.4 us (0.53); the launches traced: 182 us -> 96.8 us
  blocking collectives: 128 us -> 35.8 us
  waiting for transfers between devices: 8.74 us -> 26.5 us
  Pallas kernels: 0 us -> 11.5 us
  matrix products: 10.6 us -> 0 us
  local copies, waits for them, and re-layouts: 19.3 us -> 11.6 us
  other arithmetic: 6.47 us -> 0 us
    all_to_all x4 -> x1, blocking collectives: 98.5 us -> 35.8 us  [exchange(): lax.all_to_all(block.reshape(devices, capacity, model_width), ('exp', 'se...]
    all_gather x2 -> x0, blocking collectives: 29 us -> none  [the longest x1 18.2 us: per_device(): lax.all_gather(keys, 'seq', axis=0, tiled=True)]
    all_to_all x2 -> x1, waiting for transfers between devices: 8.74 us -> 26.2 us  [exchange(): lax.all_to_all(block.reshape(devices, capacity, model_width), ('exp', 'se...]
    pallas_call x0 -> x3, Pallas kernels: none -> 11.5 us  [the longest x1 5.32 us: experts(): pl.pallas_call(expert_kernel, grid=(steps,), out_shape=jax.ShapeDtypeStru...]
    dot_general x6 -> x0, matrix products: 10.6 us -> none  [the longest x1 4.56 us: expert_parts(): jnp.einsum('rd,qdf->qrf', rows_in, stack_in, preferred_element_type=jnp.f...]
    ppermute x0 -> x2, starting transfers between devices: none -> 8.25 us  [per_device(): lax.ppermute(own, 'seq', [(i, i + hop) for i in range(seq_count - hop)])]
    unnamed x14 -> x17, local copies, waits for them, and re-layouts: 1.93 us -> 8.96 us
    all_to_all x2 -> x1, starting transfers between devices: 9.56 us -> 3.17 us  [exchange(): lax.all_to_all(block.reshape(devices, capacity, model_width), ('exp', 'se...]
  transfers between devices with their start and end apart: 2 -> 3, of which waited for: 1 -> 2; matrix products, arithmetic and copies ran while one was open for 5% -> 2% of each run, Pallas kernels for 0% -> 0%
where the time goes in v1:
time: 97.4 us; the launch traced here: 96.8 us
  blocking collectives  35.8 us (37%)
  waiting for transfers between devices  26.5 us (27%)
  local copies, waits for them, and re-layouts  11.6 us (12%)
  Pallas kernels  11.5 us (12%)
  starting transfers between devices  11.4 us (12%)
    all_to_all x1, blocking collectives, exchange(): lax.all_to_all(block.reshape(devices, capacity, model_width), ('exp', 'se...  35.8 us
    all_to_all x1, waiting for transfers between devices, exchange(): lax.all_to_all(block.reshape(devices, capacity, model_width), ('exp', 'se...  26.2 us
    unnamed x17, local copies, waits for them, and re-layouts  8.96 us
    ppermute x2, starting transfers between devices, per_device(): lax.ppermute(own, 'seq', [(i, i + hop) for i in range(seq_count - hop)])  8.25 us
    pallas_call x1, Pallas kernels, experts(): pl.pallas_call(expert_kernel, grid=(steps,), out_shape=jax.ShapeDtypeStru...  5.32 us
    pallas_call x1, Pallas kernels, attend(): pl.pallas_call(functools.partial(attend_kernel, blocks, splits, capacity)...  4.83 us
    all_to_all x1, starting transfers between devices, exchange(): lax.all_to_all(block.reshape(devices, capacity, model_width), ('exp', 'se...  3.17 us
  transfers between devices with their start and end apart: 3, of which 2 were waited for; matrix products, arithmetic and copies ran while one was open for 2% of the time, Pallas kernels for 0%

profile of v1, /device:TPU:1, one launch (start us, length us, event | category | flops | bytes accessed | tf_op | source)
XLA Modules:
  0.0 96.8 jit_solution(6435934716169159075)
XLA Ops:
  0.0 0.8 constant_dynamic-update-slice_fusion.1
  0.8 0.8 constant_dynamic-update-slice_fusion.refs_2_
  1.7 5.0 %collective-permute-start = (bf16[128,512]{1,0:T(8,128)(2,1)S(1)}, bf16[128,512]{1,0:T(8,128)(2,1)S(1)}, u32[]{:S(2)}, u32[]{:S(2)}) collective-permute-start(bf16[128,512]{1,0:T(8,128)(2,1)S(1)} %constant_dynamic-update-slice_fusion.refs_2_), channel_id=1, source_target_pairs={{0,2},{1,3},{4,6},{5,7},{8,10},{9,11},{12,14},{13,15},{16,18},{17,... | collective-permute-start | bytes 393224 | tf_op jit(solution)/shard_map/ppermute | solution.py:188
  6.7 3.2 %collective-permute-start.1 = (bf16[128,512]{1,0:T(8,128)(2,1)S(1)}, bf16[128,512]{1,0:T(8,128)(2,1)S(1)}, u32[]{:S(2)}, u32[]{:S(2)}) collective-permute-start(bf16[128,512]{1,0:T(8,128)(2,1)S(1)} %constant_dynamic-update-slice_fusion.refs_2_), channel_id=1, source_target_pairs={{0,1},{1,2},{2,3},{4,5},{5,6},{6,7},{8,9},{9,10},{10,11},{12,13},{... | collective-permute-start | bytes 393224 | tf_op jit(solution)/shard_map/ppermute | solution.py:188
  10.0 0.8 pad_dynamic-slice_fusion
  10.7 0.1 copy.11.refs_3_
  10.8 0.8 copy.12.refs_7_.ids_col_ref
  11.6 0.0 collective-permute-done.refs_0_
  11.6 0.3 collective-permute-done.1.refs_1_
  11.9 1.0 %copy-done.2 = bf16[128,2048]{1,0:T(8,128)(2,1)S(1)} copy-done((bf16[128,2048]{1,0:T(8,128)(2,1)S(1)}, bf16[128,2048]{1,0:T(8,128)(2,1)}, u32[]{:S(2)}) %copy-start.2) | copy-done | bytes 524312
  12.9 1.0 %copy-done.3 = bf16[128,2048]{1,0:T(8,128)(2,1)S(1)} copy-done((bf16[128,2048]{1,0:T(8,128)(2,1)S(1)}, bf16[128,2048]{1,0:T(8,128)(2,1)}, u32[]{:S(2)}) %copy-start.3) | copy-done | bytes 524312
  14.0 0.7 copy-done.4
  14.7 0.7 copy-done.5
  15.3 4.8 %attend.1 = (bf16[128,2048]{1,0:T(8,128)(2,1)S(1)}, bf16[256,2048]{1,0:T(8,128)(2,1)S(1)}) custom-call(bf16[128,2048]{1,0:T(8,128)(2,1)S(1)} %copy-done.2, bf16[128,512]{1,0:T(8,128)(2,1)S(1)} %collective-permute-done.refs_0_, bf16[128,512]{1,0:T(8,128)(2,1)S(1)} %collective-permute-done.1.refs_1_, ...), custom_call_target="tpu_custom_call" | custom-call | tf_op jit(solution)/shard_map/attend/pallas_call | solution.py:78
  20.1 35.8 %all_to_all.10 = bf16[32,8,2048]{2,1,0:T(8,128)(2,1)S(1)} all-to-all(bf16[32,8,2048]{2,1,0:T(8,128)(2,1)S(1)} %bitcast.12), channel_id=1, replica_groups=mesh['exp'=8,'seq'=4] {'exp','seq'}, dimensions={0} | all-to-all | bytes 2097152 | tf_op jit(solution)/shard_map/all_to_all | solution.py:199
  55.9 2.8 %copy-done = bf16[1,2048,1536]{2,1,0:T(8,128)(2,1)S(1)} copy-done((bf16[1,2048,1536]{2,1,0:T(8,128)(2,1)S(1)}, bf16[1,2048,1536]{2,1,0:T(8,128)(2,1)}, u32[]{:S(2)}) %copy-start) | copy-done | bytes 6291480
  58.7 1.9 %copy-done.1 = bf16[1,768,2048]{2,1,0:T(8,128)(2,1)S(1)} copy-done((bf16[1,768,2048]{2,1,0:T(8,128)(2,1)S(1)}, bf16[1,768,2048]{2,1,0:T(8,128)(2,1)}, u32[]{:S(2)}) %copy-start.1) | copy-done | bytes 3145752
  60.6 5.3 %experts.1 = bf16[256,2048]{1,0:T(8,128)(2,1)} custom-call(bf16[256,2048]{1,0:T(8,128)(2,1)S(1)} %bitcast.10, bf16[1,2048,1536]{2,1,0:T(8,128)(2,1)S(1)} %copy-done, bf16[1,2048,1536]{2,1,0:T(8,128)(2,1)S(1)} %copy-done, bf16[1,768,2048]{2,1,0:T(8,128)(2,1)S(1)} %copy-done.1), custom_call_target="tpu_custom_call" | custom-call | tf_op jit(solution)/shard_map/experts/pallas_call | solution.py:121
  65.9 3.2 %all-to-all-start.1 = ((bf16[32,8,2048]{2,1,0:T(8,128)(2,1)}), bf16[32,8,2048]{2,1,0:T(8,128)(2,1)S(1)}, u32[]{:S(2)}, u32[]{:S(2)}) async-start(bf16[32,8,2048]{2,1,0:T(8,128)(2,1)} %bitcast.6), calls=%async_computation.1 | async-start | bytes 2097152 | tf_op jit(solution)/shard_map/all_to_all | solution.py:199
  69.1 0.0 copy-done.7
  69.1 0.1 copy.13.gate_ref
  69.2 26.2 %all-to-all-done.1 = bf16[32,8,2048]{2,1,0:T(8,128)(2,1)S(1)} async-done(((bf16[32,8,2048]{2,1,0:T(8,128)(2,1)}), bf16[32,8,2048]{2,1,0:T(8,128)(2,1)S(1)}, u32[]{:S(2)}, u32[]{:S(2)}) %all-to-all-start.1) | async-done | bytes 1048608 | tf_op jit(solution)/shard_map/all_to_all | solution.py:199
  95.4 0.0 copy-done.6
  95.4 1.3 %combine.1 = bf16[128,2048]{1,0:T(8,128)(2,1)} custom-call(bf16[256,2048]{1,0:T(8,128)(2,1)S(1)} %bitcast.11, bf16[128,2048]{1,0:T(8,128)(2,1)S(1)} %get-tuple-element.8.hidden_ref, f32[128,1]{1,0:T(8,128)S(1)} %copy.13.gate_ref, s32[128,1]{1,0:T(8,128)S(1)} %copy.12.refs_7_.ids_col_ref, s32[1,128]{1,0:T(1,128)S(1)} %bitcast.16), custom_call_target="tpu_custom_call" | custom-call | tf_op jit(solution)/shard_map/combine/pallas_call | solution.py:161
  (10 shorter events, 0.0 us)
Async XLA Ops:
  1.7 9.9 %collective-permute-start = (bf16[128,512]{1,0:T(8,128)(2,1)S(1)}, bf16[128,512]{1,0:T(8,128)(2,1)S(1)}, u32[]{:S(2)}, u32[]{:S(2)}) collective-permute-start(bf16[128,512]{1,0:T(8,128)(2,1)S(1)} %constant_dynamic-update-slice_fusion.refs_2_), channel_id=1, source_target_pairs={{0,2},{1,3},{4,6},{5,7},{8,10},{9,11},{12,14},{13,15},{16,18},{17,... | collective-permute-start | bytes 393224 | tf_op jit(solution)/shard_map/ppermute | solution.py:188
  6.7 5.1 %collective-permute-start.1 = (bf16[128,512]{1,0:T(8,128)(2,1)S(1)}, bf16[128,512]{1,0:T(8,128)(2,1)S(1)}, u32[]{:S(2)}, u32[]{:S(2)}) collective-permute-start(bf16[128,512]{1,0:T(8,128)(2,1)S(1)} %constant_dynamic-update-slice_fusion.refs_2_), channel_id=1, source_target_pairs={{0,1},{1,2},{2,3},{4,5},{5,6},{6,7},{8,9},{9,10},{10,11},{12,13},{... | collective-permute-start | bytes 393224 | tf_op jit(solution)/shard_map/ppermute | solution.py:188
  11.9 1.0 %copy-start.2 = (bf16[128,2048]{1,0:T(8,128)(2,1)S(1)}, bf16[128,2048]{1,0:T(8,128)(2,1)}, u32[]{:S(2)}) copy-start(bf16[128,2048]{1,0:T(8,128)(2,1)} %q_ref.1) | copy-start | bytes 1572868
  12.9 1.0 %copy-start.3 = (bf16[128,2048]{1,0:T(8,128)(2,1)S(1)}, bf16[128,2048]{1,0:T(8,128)(2,1)}, u32[]{:S(2)}) copy-start(bf16[128,2048]{1,0:T(8,128)(2,1)} %refs_5_.1) | copy-start | bytes 1572868
  14.0 0.7 copy-start.4
  14.7 0.7 copy-start.5
  55.9 2.8 %copy-start = (bf16[1,2048,1536]{2,1,0:T(8,128)(2,1)S(1)}, bf16[1,2048,1536]{2,1,0:T(8,128)(2,1)}, u32[]{:S(2)}) copy-start(bf16[1,2048,1536]{2,1,0:T(8,128)(2,1)} %up_ref.1) | copy-start | bytes 18874372
  58.7 1.9 %copy-start.1 = (bf16[1,768,2048]{2,1,0:T(8,128)(2,1)S(1)}, bf16[1,768,2048]{2,1,0:T(8,128)(2,1)}, u32[]{:S(2)}) copy-start(bf16[1,768,2048]{2,1,0:T(8,128)(2,1)} %down_ref.1) | copy-start | bytes 9437188
  60.6 8.5 %copy-start.7 = (f32[128]{0:T(128)S(1)}, f32[128]{0:T(128)}, u32[]{:S(2)}) copy-start(f32[128]{0:T(128)} %param.17) | copy-start | bytes 1540
  60.6 34.9 %copy-start.6 = (s32[128]{0:T(128)S(1)}, s32[128]{0:T(128)}, u32[]{:S(2)}) copy-start(s32[128]{0:T(128)} %param.16) | copy-start | bytes 1540
  65.9 29.5 %all-to-all-start.1 = ((bf16[32,8,2048]{2,1,0:T(8,128)(2,1)}), bf16[32,8,2048]{2,1,0:T(8,128)(2,1)S(1)}, u32[]{:S(2)}, u32[]{:S(2)}) async-start(bf16[32,8,2048]{2,1,0:T(8,128)(2,1)} %bitcast.6), calls=%async_computation.1 | async-start | bytes 2097152 | tf_op jit(solution)/shard_map/all_to_all | solution.py:199

commit v2 on v1

v2 whole, which is shorter than its diff:
```python
import functools
import math

import jax
import jax.numpy as jnp
from jax import lax
from jax.experimental import pallas as pl
from jax.experimental.pallas import tpu as pltpu
from jax.sharding import PartitionSpec as P

HD = 128
HEADS = 16
KVH = 2
EXP_DEV = 4
FF = 768
EPS = 1e-6
F32 = jnp.float32
BF16 = jnp.bfloat16
VMEM = pl.BlockSpec(memory_space=pltpu.VMEM)
HBM = pl.BlockSpec(memory_space=pltpu.HBM)
SCALE = 1.0 / math.sqrt(HD)
GROUP = HEADS // KVH
MIB = 2**20


def head_cols(head):
    return slice(head * HD, (head + 1) * HD)


def iota(shape, dimension):
    return lax.broadcasted_iota(jnp.int32, shape, dimension)


def as_column(row):
    count = row.shape[1]
    square = jnp.broadcast_to(row, (count, count))
    eye = iota((count, count), 0) == iota((count, count), 1)
    kept = jnp.where(eye, square, jnp.zeros_like(square))
    if row.dtype == jnp.int32:
        return jnp.sum(kept.astype(F32), axis=1, keepdims=True).astype(jnp.int32)
    return jnp.sum(kept, axis=1, keepdims=True)


def stage_kernel(before, splits, capacity, *refs):
    count = 7
    sources, refs = refs[:count], refs[count:]
    copied, refs = refs[: count - 3], refs[count - 3 :]
    bias_ref, placing_ref, picking_ref, gates_ref, refs = *refs[:4], refs[4:]
    small, sems = refs[:3], refs[3]
    copies = [
        pltpu.make_async_copy(source, target, sems.at[i])
        for i, (source, target) in enumerate(zip(sources, (*small, *copied)))
    ]
    for copy in copies:
        copy.start()
    seg_ref, ids_ref, gate_row_ref = small
    for copy in copies[:3]:
        copy.wait()
    rows = bias_ref.shape[1]
    place = lax.axis_index("seq")

    def segments(hop):
        at = pl.multiple_of(jnp.maximum(place - hop, 0) * rows, rows)
        return jnp.where(place >= hop, seg_ref[:, pl.ds(at, rows)], -1)

    seg_q = segments(0)
    for block, hop in enumerate(range(before, -1, -1)):
        allowed = as_column(segments(hop)) == seg_q
        if hop == 0:
            allowed = allowed & (iota((rows, rows), 0) <= iota((rows, rows), 1))
        bias_ref[block * rows : (block + 1) * rows, :] = jnp.where(allowed, 0.0, -jnp.inf)
    slots = placing_ref.shape[0]
    ids_row = ids_ref[...]
    first = slots_of(ids_row, splits, capacity, 1)
    placing_ref[...] = one_hot(first, iota((slots, rows), 0), splits, capacity)
    first = slots_of(ids_row, splits, capacity, 0)
    picking_ref[...] = one_hot(first, iota((rows, slots), 1), splits, capacity)
    gates_ref[...] = jnp.broadcast_to(as_column(gate_row_ref[...]), gates_ref.shape)
    for copy in copies[3:]:
        copy.wait()


def stage(before, splits, capacity, slots, seg, ids, gates, *large):
    rows = large[0].shape[0]
    sources = (seg, ids, gates, *large)
    return pl.pallas_call(
        functools.partial(stage_kernel, before, splits, capacity),
        out_shape=(
            *[pltpu.VMEM(array.shape, array.dtype) for array in large],
            pltpu.VMEM(((before + 1) * rows, rows), F32),
            pltpu.VMEM((slots, rows), BF16),
            pltpu.VMEM((rows, slots), BF16),
            pltpu.VMEM((rows, rows), F32),
        ),
        in_specs=[HBM] * len(sources),
        out_specs=(VMEM,) * (len(large) + 4),
        scratch_shapes=[
            *[pltpu.VMEM(array.shape, array.dtype) for array in (seg, ids, gates)],
            pltpu.SemaphoreType.DMA((len(sources),)),
        ],
        compiler_params=pltpu.CompilerParams(vmem_limit_bytes=16 * MIB),
        cost_estimate=pl.CostEstimate(flops=0, bytes_accessed=10 * MIB, transcendentals=0),
        name="stage",
    )(*[pltpu.with_memory_space_constraint(array, pltpu.HBM) for array in sources])


def slots_of(ids_row, splits, capacity, axis):
    count = ids_row.shape[1]
    ids_col = as_column(ids_row)
    earlier = iota((count, count), 1 - axis) < iota((count, count), axis)
    same = ((ids_col == ids_row) & earlier).astype(F32)
    rank = jnp.sum(same, axis=1 - axis, keepdims=True).astype(jnp.int32)
    return (ids_row if axis == 1 else ids_col) * (splits * capacity) + rank


def one_hot(first, slot_at, splits, capacity):
    hot = slot_at == first
    for split in range(1, splits):
        hot = hot | (slot_at == first + split * capacity)
    return hot.astype(F32).astype(BF16)


def attend_kernel(blocks, *refs):
    key_refs, value_refs, refs = refs[:blocks], refs[blocks : 2 * blocks], refs[2 * blocks :]
    q_ref, resid_ref, gain_ref, bias_ref, placing_ref, hidden_ref, outgoing_ref = refs[:7]
    score_ref, weight_ref, turn_ref = refs[7:]
    rows = q_ref.shape[0]
    eye = (iota((rows, rows), 0) == iota((rows, rows), 1)).astype(F32).astype(BF16)
    by_rows = (((1,), (1,)), ((), ()))
    pairs = HEADS // 2
    kv_of = [2 * pair // GROUP for pair in range(pairs)]
    bias = jnp.concatenate([bias_ref[...]] * 2, 1)
    head_keys = [
        jnp.concatenate([ref[:, head_cols(kv_head)] for ref in key_refs], 0)
        for kv_head in range(KVH)
    ]
    for pair in range(pairs):
        pair_queries = jnp.concatenate([q_ref[:, head_cols(2 * pair + i)] for i in range(2)], 0)
        products = lax.dot_general(
            head_keys[kv_of[pair]], pair_queries, by_rows, preferred_element_type=F32
        )
        score_ref[pair] = products * SCALE + bias
    values_t = [
        jnp.concatenate(
            [
                lax.dot_general(
                    eye,
                    ref[:, head_cols(ref.shape[1] // HD - KVH + kv_head)],
                    by_rows,
                    preferred_element_type=F32,
                ).astype(BF16)
                for ref in value_refs
            ],
            1,
        )
        for kv_head in range(KVH)
    ]
    totals = []
    for pair in range(pairs):
        scores = score_ref[pair]
        weights = jnp.exp(scores - jnp.max(scores, axis=0, keepdims=True))
        totals.append(jnp.sum(weights, axis=0, keepdims=True))
        weight_ref[pair] = weights.astype(BF16)
    for pair in range(pairs):
        mixture = jnp.dot(values_t[kv_of[pair]], weight_ref[pair], preferred_element_type=F32)
        attended = (mixture * (1.0 / totals[pair])).astype(BF16)
        for i in range(2):
            turn_ref[head_cols(2 * pair + i), :] = attended[:, i * rows : (i + 1) * rows]
    step = 512
    squares = jnp.zeros((rows, HD), F32)
    for low in range(0, HEADS * HD, step):
        cols = slice(low, low + step)
        attended = lax.dot_general(eye, turn_ref[cols, :], by_rows, preferred_element_type=F32)
        hidden = (resid_ref[:, cols].astype(F32) + attended).astype(BF16)
        hidden_ref[:, cols] = hidden
        hidden_float = hidden.astype(F32)
        square = hidden_float * hidden_float
        for at in range(0, step, HD):
            squares += square[:, at : at + HD]
    sumsq = jnp.sum(squares, axis=-1, keepdims=True)
    inverse = jnp.broadcast_to(lax.rsqrt(sumsq / (HEADS * HD) + EPS), (rows, step))
    placing = placing_ref[...]
    for low in range(0, HEADS * HD, step):
        cols = slice(low, low + step)
        normed = (hidden_ref[:, cols].astype(F32) * inverse * gain_ref[:, cols]).astype(BF16)
        outgoing_ref[:, cols] = jnp.dot(placing, normed, preferred_element_type=F32).astype(BF16)


def attend(keys, values, queries, resid, gain, bias, placing):
    rows, model_width = resid.shape
    slots = placing.shape[0]
    operands = (*keys, *values, queries, resid, gain, bias, placing)
    return pl.pallas_call(
        functools.partial(attend_kernel, len(keys)),
        out_shape=(
            pltpu.VMEM((rows, model_width), BF16),
            pltpu.VMEM((slots, model_width), BF16),
        ),
        in_specs=[VMEM] * len(operands),
        out_specs=(VMEM, VMEM),
        scratch_shapes=[
            pltpu.VMEM((HEADS // 2, len(keys) * rows, 2 * rows), F32),
            pltpu.VMEM((HEADS // 2, len(keys) * rows, 2 * rows), BF16),
            pltpu.VMEM((model_width, rows), BF16),
        ],
        compiler_params=pltpu.CompilerParams(vmem_limit_bytes=32 * MIB),
        name="attend",
    )(*operands)


def expert_kernel(x_ref, in_ref, down_ref, out_ref, active_ref):
    units = down_ref.shape[1]
    tile = 256
    rows_in = x_ref[...]
    for low in range(0, units, tile):
        gate = jnp.dot(rows_in, in_ref[0, :, low : low + tile], preferred_element_type=F32)
        up_cols = slice(units + low, units + low + tile)
        up = jnp.dot(rows_in, in_ref[0, :, up_cols], preferred_element_type=F32)
        active_ref[:, low : low + tile] = (gate / (1.0 + jnp.exp(-gate)) * up).astype(BF16)
    active = active_ref[...]
    step = 512
    for low in range(0, out_ref.shape[1], step):
        cols = slice(low, low + step)
        out_ref[:, cols] = jnp.dot(
            active, down_ref[0, :, cols], preferred_element_type=F32
        ).astype(BF16)


def experts(rows_in, w_in, w_out):
    rows, model_width = rows_in.shape
    units = w_out.shape[1]
    if units % 256:
        gate_up = jnp.dot(rows_in, w_in[0], preferred_element_type=F32)
        active = (jax.nn.silu(gate_up[:, :units]) * gate_up[:, units:]).astype(BF16)
        return jnp.dot(active, w_out[0], preferred_element_type=F32).astype(BF16)
    return pl.pallas_call(
        expert_kernel,
        out_shape=jax.ShapeDtypeStruct((rows, model_width), BF16),
        in_specs=[VMEM] * 3,
        out_specs=VMEM,
        scratch_shapes=[pltpu.VMEM((rows, units), BF16)],
        compiler_params=pltpu.CompilerParams(vmem_limit_bytes=16 * MIB),
        name="experts",
    )(rows_in, w_in, w_out)


def combine_kernel(delivered_ref, hidden_ref, picking_ref, gates_ref, out_ref):
    step = 512
    gates = jnp.concatenate([gates_ref[...]] * (step // gates_ref.shape[1]), 1)
    for low in range(0, hidden_ref.shape[1], step):
        cols = slice(low, low + step)
        routed = jnp.dot(picking_ref[...], delivered_ref[:, cols], preferred_element_type=F32)
        routed = routed.astype(BF16).astype(F32)
        out_ref[:, cols] = (hidden_ref[:, cols].astype(F32) + gates * routed).astype(BF16)


def combine(delivered, hidden, picking, gates):
    return pl.pallas_call(
        combine_kernel,
        out_shape=jax.ShapeDtypeStruct(hidden.shape, BF16),
        in_specs=[VMEM] * 4,
        out_specs=VMEM,
        compiler_params=pltpu.CompilerParams(vmem_limit_bytes=16 * MIB),
        name="combine",
    )(delivered, hidden, picking, gates)


def per_device(
    queries, keys, values, resid, seg_ids, norm_gain, expert_ids, gate_weights, w_in, w_out
):
    seq_count = lax.axis_size("seq")
    exp_count = lax.axis_size("exp")
    devices = seq_count * exp_count
    rows, model_width = resid.shape
    length = rows * seq_count
    splits = FF // w_out.shape[1]
    capacity = max(2, 2 * rows * splits // devices)
    slots = devices * capacity
    reach = length // 2
    before = min(seq_count - 1, -(-(reach - 1) // rows))

    own = jnp.concatenate([keys, values], axis=1)
    blocks = [
        lax.ppermute(own, "seq", [(i, i + hop) for i in range(seq_count - hop)])
        for hop in range(before, 0, -1)
    ]
    queries, resid, w_in, w_out, bias, placing, picking, gates = stage(
        before, splits, capacity, slots, seg_ids[None], expert_ids[None], gate_weights[None],
        queries, resid, w_in, w_out,
    )
    hidden, outgoing = attend([*blocks, keys], [*blocks, values], queries, resid, norm_gain[None], bias, placing)

    def exchange(block):
        return lax.all_to_all(
            block.reshape(devices, capacity, model_width),
            ("exp", "seq"),
            split_axis=0,
            concat_axis=0,
            tiled=True,
        ).reshape(slots, model_width)

    delivered = exchange(experts(exchange(outgoing), w_in, w_out))
    return combine(delivered, hidden, picking, gates)


def solution(mesh):
    placed = (
        P(("exp", "seq"), None),
        P(("exp", "seq"), None),
        P(("exp", "seq"), None),
        P(("exp", "seq"), None),
        P("exp"),
        P(),
        P(("exp", "seq")),
        P(("exp", "seq")),
        P(("exp", "seq"), None, None),
        P(("exp", "seq"), None, None),
    )
    return jax.shard_map(
        per_device, mesh=mesh, in_specs=placed, out_specs=P(("exp", "seq"), None), check_vma=False
    )
```

time: 97.4 us -> 83.3 us (0.86)
  blocking collectives: 35.8 us -> 62.8 us
  waiting for transfers between devices: 26.5 us -> 0.01 us
  local copies, waits for them, and re-layouts: 11.6 us -> 1.76 us
  starting transfers between devices: 11.4 us -> 8.24 us
  Pallas kernels: 11.5 us -> 10.1 us
    all_to_all x1 -> x2, blocking collectives: 35.8 us -> 62.8 us  [exchange(): lax.all_to_all(block.reshape(devices, capacity, model_width), ('exp', 'se...]
    all_to_all x1 -> x0, waiting for transfers between devices: 26.2 us -> none  [exchange(): lax.all_to_all(block.reshape(devices, capacity, model_width), ('exp', 'se...]
    unnamed x17 -> x7, local copies, waits for them, and re-layouts: 8.96 us -> 0.92 us
    all_to_all x1 -> x0, starting transfers between devices: 3.17 us -> none  [exchange(): lax.all_to_all(block.reshape(devices, capacity, model_width), ('exp', 'se...]
    pallas_call x3 -> x4, Pallas kernels: 11.5 us -> 10.1 us  [the longest x1 4.13 us: stage(): pl.pallas_call(functools.partial(stage_kernel, before, splits, capacity),...]
    broadcast_in_dim x5 -> x0, local copies, waits for them, and re-layouts: 1 us -> none  [the longest x1 0.76 us: attend(): ids[:, None]]
  transfers between devices with their start and end apart: 3 -> 2, of which waited for: 2 -> 0; matrix products, arithmetic and copies ran while one was open for 2% -> 0% of each run, Pallas kernels for 0% -> 5%
where the time goes in v2:
time: 83.3 us; the launch traced here: 83 us
  blocking collectives  62.8 us (75%)
  Pallas kernels  10.1 us (12%)
  starting transfers between devices  8.24 us (10%)
  local copies, waits for them, and re-layouts  1.76 us (2%)
    all_to_all x2, blocking collectives, exchange(): lax.all_to_all(block.reshape(devices, capacity, model_width), ('exp', 'se...  62.8 us
    ppermute x2, starting transfers between devices, per_device(): lax.ppermute(own, 'seq', [(i, i + hop) for i in range(seq_count - hop)])  8.24 us
    pallas_call x1, Pallas kernels, stage(): pl.pallas_call(functools.partial(stage_kernel, before, splits, capacity),...  4.13 us
    pallas_call x1, Pallas kernels, experts(): pl.pallas_call(expert_kernel, out_shape=jax.ShapeDtypeStruct((rows, model...  2.63 us
    pallas_call x1, Pallas kernels, attend(): pl.pallas_call(functools.partial(attend_kernel, len(keys)), out_shape=(pl...  2.23 us
  transfers between devices with their start and end apart: 2, of which 0 were waited for; matrix products, arithmetic and copies ran while one was open for 0% of the time, Pallas kernels for 5%

profile of v2, /device:TPU:1, one launch (start us, length us, event | category | flops | bytes accessed | tf_op | source)
XLA Modules:
  0.0 83.0 jit_solution(7033284977300090463)
XLA Ops:
  0.0 0.0 copy-start
  0.0 0.0 copy-start.1
  0.0 0.0 copy-start.2
  0.0 0.9 %constant_dynamic-update-slice_fusion.1 = bf16[128,512]{1,0:T(8,128)(2,1)S(1)} fusion(bf16[128,256]{1,0:T(8,128)(2,1)} %refs_2_.1), kind=kLoop, calls=%fused_computation.1 | loop fusion | bytes 131072
  0.9 0.8 %constant_dynamic-update-slice_fusion = bf16[128,512]{1,0:T(8,128)(2,1)S(1)} fusion(bf16[128,512]{1,0:T(8,128)(2,1)S(1)} %constant_dynamic-update-slice_fusion.1, bf16[128,256]{1,0:T(8,128)(2,1)} %refs_5_.3), kind=kLoop, calls=%fused_computation | loop fusion | bytes 131072 | tf_op jit(solution)/shard_map/concatenate | solution.py:282
  1.8 4.0 %collective-permute-start.1 = (bf16[128,512]{1,0:T(8,128)(2,1)S(1)}, bf16[128,512]{1,0:T(8,128)(2,1)S(1)}, u32[]{:S(2)}, u32[]{:S(2)}) collective-permute-start(bf16[128,512]{1,0:T(8,128)(2,1)S(1)} %constant_dynamic-update-slice_fusion), channel_id=1, source_target_pairs={{0,1},{1,2},{2,3},{4,5},{5,6},{6,7},{8,9},{9,10},{10,11},{12,13},{... | collective-permute-start | bytes 393224 | tf_op jit(solution)/shard_map/ppermute | solution.py:284
  5.8 4.2 %collective-permute-start = (bf16[128,512]{1,0:T(8,128)(2,1)S(1)}, bf16[128,512]{1,0:T(8,128)(2,1)S(1)}, u32[]{:S(2)}, u32[]{:S(2)}) collective-permute-start(bf16[128,512]{1,0:T(8,128)(2,1)S(1)} %constant_dynamic-update-slice_fusion), channel_id=1, source_target_pairs={{0,2},{1,3},{4,6},{5,7},{8,10},{9,11},{12,14},{13,15},{16,18},{17,... | collective-permute-start | bytes 393224 | tf_op jit(solution)/shard_map/ppermute | solution.py:284
  10.0 4.1 %stage.1 = (bf16[128,2048]{1,0:T(8,128)(2,1)S(1)}, bf16[128,2048]{1,0:T(8,128)(2,1)S(1)}, bf16[1,2048,1536]{2,1,0:T(8,128)(2,1)S(1)}, bf16[1,768,2048]{2,1,0:T(8...) custom-call(s32[1,512]{1,0:T(1,128)} %bitcast.13, ...), custom_call_target="tpu_custom_call" | custom-call | bytes 10485760 | tf_op jit(solution)/shard_map/stage/pallas_call | solution.py:86
  14.2 0.0 collective-permute-done.1.refs_1_.refs_4_
  14.2 0.0 collective-permute-done.refs_0_.refs_3_
  14.2 0.0 copy-done
  14.2 0.0 copy-done.1
  14.2 0.0 copy-done.2
  14.2 2.2 %attend.1 = (bf16[128,2048]{1,0:T(8,128)(2,1)S(1)}, bf16[256,2048]{1,0:T(8,128)(2,1)S(1)}) custom-call(bf16[128,512]{1,0:T(8,128)(2,1)S(1)} %collective-permute-done.refs_0_.refs_3_, bf16[128,512]{1,0:T(8,128)(2,1)S(1)} %collective-permute-done.1.refs_1_.refs_4_, bf16[128,256]{1,0:T(8,128)(2,1)S(1)} %copy-done, ...), custom_call_target="tpu_custom_call" | custom-call | tf_op jit(solution)/shard_map/attend/pallas_call | solution.py:193
  16.4 33.4 %all_to_all.10 = bf16[32,8,2048]{2,1,0:T(8,128)(2,1)S(1)} all-to-all(bf16[32,8,2048]{2,1,0:T(8,128)(2,1)S(1)} %bitcast.11), channel_id=1, replica_groups=mesh['exp'=8,'seq'=4] {'exp','seq'}, dimensions={0} | all-to-all | bytes 2097152 | tf_op jit(solution)/shard_map/all_to_all | solution.py:294
  49.9 2.6 %experts.1 = bf16[256,2048]{1,0:T(8,128)(2,1)S(1)} custom-call(bf16[256,2048]{1,0:T(8,128)(2,1)S(1)} %bitcast.9, bf16[1,2048,1536]{2,1,0:T(8,128)(2,1)S(1)} %get-tuple-element.20.in_ref, bf16[1,768,2048]{2,1,0:T(8,128)(2,1)S(1)} %get-tuple-element.21.down_ref), custom_call_target="tpu_custom_call" | custom-call | tf_op jit(solution)/shard_map/experts/pallas_call | solution.py:236
  52.5 29.3 %all_to_all.11 = bf16[32,8,2048]{2,1,0:T(8,128)(2,1)S(1)} all-to-all(bf16[32,8,2048]{2,1,0:T(8,128)(2,1)S(1)} %bitcast.10), channel_id=1, replica_groups=mesh['exp'=8,'seq'=4] {'exp','seq'}, dimensions={0} | all-to-all | bytes 2097152 | tf_op jit(solution)/shard_map/all_to_all | solution.py:294
  81.8 1.1 %combine.1 = bf16[128,2048]{1,0:T(8,128)(2,1)} custom-call(bf16[256,2048]{1,0:T(8,128)(2,1)S(1)} %bitcast.8, bf16[128,2048]{1,0:T(8,128)(2,1)S(1)} %get-tuple-element.22.hidden_ref, bf16[128,256]{1,0:T(8,128)(2,1)S(1)} %get-tuple-element.23.picking_ref, f32[128,128]{1,0:T(8,128)S(1)} %get-tuple-element.24.gates_ref), custom_call_target="tpu_custom_call" | custom-call | tf_op jit(solution)/shard_map/combine/pallas_call | solution.py:258
Async XLA Ops:
  0.0 14.2 %copy-start = (bf16[128,256]{1,0:T(8,128)(2,1)S(1)}, bf16[128,256]{1,0:T(8,128)(2,1)}, u32[]{:S(2)}) copy-start(bf16[128,256]{1,0:T(8,128)(2,1)} %refs_2_.1) | copy-start | bytes 196612
  0.0 14.2 %copy-start.1 = (bf16[128,256]{1,0:T(8,128)(2,1)S(1)}, bf16[128,256]{1,0:T(8,128)(2,1)}, u32[]{:S(2)}) copy-start(bf16[128,256]{1,0:T(8,128)(2,1)} %refs_5_.3) | copy-start | bytes 196612
  0.0 14.2 %copy-start.2 = (f32[2048]{0:T(1024)S(1)}, f32[2048]{0:T(1024)}, u32[]{:S(2)}) copy-start(f32[2048]{0:T(1024)} %param.15) | copy-start | bytes 24580
  1.8 12.4 %collective-permute-start.1 = (bf16[128,512]{1,0:T(8,128)(2,1)S(1)}, bf16[128,512]{1,0:T(8,128)(2,1)S(1)}, u32[]{:S(2)}, u32[]{:S(2)}) collective-permute-start(bf16[128,512]{1,0:T(8,128)(2,1)S(1)} %constant_dynamic-update-slice_fusion), channel_id=1, source_target_pairs={{0,1},{1,2},{2,3},{4,5},{5,6},{6,7},{8,9},{9,10},{10,11},{12,13},{... | collective-permute-start | bytes 393224 | tf_op jit(solution)/shard_map/ppermute | solution.py:284
  5.8 8.4 %collective-permute-start = (bf16[128,512]{1,0:T(8,128)(2,1)S(1)}, bf16[128,512]{1,0:T(8,128)(2,1)S(1)}, u32[]{:S(2)}, u32[]{:S(2)}) collective-permute-start(bf16[128,512]{1,0:T(8,128)(2,1)S(1)} %constant_dynamic-update-slice_fusion), channel_id=1, source_target_pairs={{0,2},{1,3},{4,6},{5,7},{8,10},{9,11},{12,14},{13,15},{16,18},{17,... | collective-permute-start | bytes 393224 | tf_op jit(solution)/shard_map/ppermute | solution.py:284

commit v3 on v2

--- a/solution.py
+++ b/solution.py
@@ -21,6 +21,8 @@
 SCALE = 1.0 / math.sqrt(HD)
 GROUP = HEADS // KVH
 MIB = 2**20
+PAIRS = HEADS // 2
+BY_ROWS = (((1,), (1,)), ((), ()))
 
 
 def head_cols(head):
@@ -120,57 +122,73 @@
     return hot.astype(F32).astype(BF16)
 
 
-def attend_kernel(blocks, *refs):
-    key_refs, value_refs, refs = refs[:blocks], refs[blocks : 2 * blocks], refs[2 * blocks :]
-    q_ref, resid_ref, gain_ref, bias_ref, placing_ref, hidden_ref, outgoing_ref = refs[:7]
-    score_ref, weight_ref, turn_ref = refs[7:]
-    rows = q_ref.shape[0]
-    eye = (iota((rows, rows), 0) == iota((rows, rows), 1)).astype(F32).astype(BF16)
-    by_rows = (((1,), (1,)), ((), ()))
-    pairs = HEADS // 2
-    kv_of = [2 * pair // GROUP for pair in range(pairs)]
+def weigh_kernel(blocks, *refs):
+    key_refs, (q_ref, bias_ref, weight_ref, totals_ref, score_ref) = refs[:blocks], refs[blocks:]
     bias = jnp.concatenate([bias_ref[...]] * 2, 1)
     head_keys = [
         jnp.concatenate([ref[:, head_cols(kv_head)] for ref in key_refs], 0)
         for kv_head in range(KVH)
     ]
-    for pair in range(pairs):
+    for pair in range(PAIRS):
         pair_queries = jnp.concatenate([q_ref[:, head_cols(2 * pair + i)] for i in range(2)], 0)
         products = lax.dot_general(
-            head_keys[kv_of[pair]], pair_queries, by_rows, preferred_element_type=F32
+            head_keys[2 * pair // GROUP], pair_queries, BY_ROWS, preferred_element_type=F32
         )
         score_ref[pair] = products * SCALE + bias
+    for pair in range(PAIRS):
+        scores = score_ref[pair]
+        weights = jnp.exp(scores - jnp.max(scores, axis=0, keepdims=True))
+        totals_ref[pair : pair + 1, :] = jnp.sum(weights, axis=0, keepdims=True)
+        weight_ref[pair] = weights.astype(BF16)
+
+
+def weigh(keys, queries, bias):
+    rows = queries.shape[0]
+    shape = (PAIRS, len(keys) * rows, 2 * rows)
+    operands = (*keys, queries, bias)
+    return pl.pallas_call(
+        functools.partial(weigh_kernel, len(keys)),
+        out_shape=(pltpu.VMEM(shape, BF16), pltpu.VMEM((PAIRS, 2 * rows), F32)),
+        in_specs=[VMEM] * len(operands),
+        out_specs=(VMEM, VMEM),
+        scratch_shapes=[pltpu.VMEM(shape, F32)],
+        compiler_params=pltpu.CompilerParams(vmem_limit_bytes=24 * MIB),
+        cost_estimate=pl.CostEstimate(
+            flops=4 * len(keys) * rows * rows * HEADS * HD, bytes_accessed=MIB, transcendentals=0
+        ),
+        name="weigh",
+    )(*operands)
+
+
+def mix_kernel(blocks, *refs):
+    value_refs, refs = refs[:blocks], refs[blocks:]
+    weight_ref, totals_ref, resid_ref, gain_ref, placing_ref = refs[:5]
+    hidden_ref, outgoing_ref, turn_ref = refs[5:]
+    rows = resid_ref.shape[0]
+    eye = (iota((rows, rows), 0) == iota((rows, rows), 1)).astype(F32).astype(BF16)
+
+    def turned(block):
+        return lax.dot_general(eye, block, BY_ROWS, preferred_element_type=F32)
+
     values_t = [
         jnp.concatenate(
-            [
-                lax.dot_general(
-                    eye,
-                    ref[:, head_cols(ref.shape[1] // HD - KVH + kv_head)],
-                    by_rows,
-                    preferred_element_type=F32,
-                ).astype(BF16)
-                for ref in value_refs
-            ],
-            1,
+            [turned(ref[:, head_cols(kv_head)]).astype(BF16) for ref in value_refs], 1
         )
         for kv_head in range(KVH)
     ]
-    totals = []
-    for pair in range(pairs):
-        scores = score_ref[pair]
-        weights = jnp.exp(scores - jnp.max(scores, axis=0, keepdims=True))
-        totals.append(jnp.sum(weights, axis=0, keepdims=True))
-        weight_ref[pair] = weights.astype(BF16)
-    for pair in range(pairs):
-        mixture = jnp.dot(values_t[kv_of[pair]], weight_ref[pair], preferred_element_type=F32)
-        attended = (mixture * (1.0 / totals[pair])).astype(BF16)
+    scale = 1.0 / totals_ref[...]
+    for pair in range(PAIRS):
+        mixture = jnp.dot(
+            values_t[2 * pair // GROUP], weight_ref[pair], preferred_element_type=F32
+        )
+        attended = (mixture * scale[pair : pair + 1, :]).astype(BF16)
         for i in range(2):
             turn_ref[head_cols(2 * pair + i), :] = attended[:, i * rows : (i + 1) * rows]
     step = 512
     squares = jnp.zeros((rows, HD), F32)
     for low in range(0, HEADS * HD, step):
         cols = slice(low, low + step)
-        attended = lax.dot_general(eye, turn_ref[cols, :], by_rows, preferred_element_type=F32)
+        attended = turned(turn_ref[cols, :])
         hidden = (resid_ref[:, cols].astype(F32) + attended).astype(BF16)
         hidden_ref[:, cols] = hidden
         hidden_float = hidden.astype(F32)
@@ -186,25 +204,20 @@
         outgoing_ref[:, cols] = jnp.dot(placing, normed, preferred_element_type=F32).astype(BF16)
 
 
-def attend(keys, values, queries, resid, gain, bias, placing):
+def mix(values, weights, totals, resid, gain, placing):
     rows, model_width = resid.shape
-    slots = placing.shape[0]
-    operands = (*keys, *values, queries, resid, gain, bias, placing)
-    return pl.pallas_call(
-        functools.partial(attend_kernel, len(keys)),
+    operands = (*values, weights, totals, resid, gain, placing)
+    return pl.pallas_call(
+        functools.partial(mix_kernel, len(values)),
         out_shape=(
             pltpu.VMEM((rows, model_width), BF16),
-            pltpu.VMEM((slots, model_width), BF16),
+            pltpu.VMEM((placing.shape[0], model_width), BF16),
         ),
         in_specs=[VMEM] * len(operands),
         out_specs=(VMEM, VMEM),
-        scratch_shapes=[
-            pltpu.VMEM((HEADS // 2, len(keys) * rows, 2 * rows), F32),
-            pltpu.VMEM((HEADS // 2, len(keys) * rows, 2 * rows), BF16),
-            pltpu.VMEM((model_width, rows), BF16),
-        ],
-        compiler_params=pltpu.CompilerParams(vmem_limit_bytes=32 * MIB),
-        name="attend",
+        scratch_shapes=[pltpu.VMEM((model_width, rows), BF16)],
+        compiler_params=pltpu.CompilerParams(vmem_limit_bytes=16 * MIB),
+        name="mix",
     )(*operands)
 
 
@@ -279,16 +292,20 @@
     reach = length // 2
     before = min(seq_count - 1, -(-(reach - 1) // rows))
 
-    own = jnp.concatenate([keys, values], axis=1)
-    blocks = [
-        lax.ppermute(own, "seq", [(i, i + hop) for i in range(seq_count - hop)])
-        for hop in range(before, 0, -1)
-    ]
+
+    def earlier(own):
+        return [
+            lax.ppermute(own, "seq", [(i, (i + hop) % seq_count) for i in range(seq_count)])
+            for hop in range(before, 0, -1)
+        ]
+
+    key_blocks, value_blocks = earlier(keys), earlier(values)
     queries, resid, w_in, w_out, bias, placing, picking, gates = stage(
         before, splits, capacity, slots, seg_ids[None], expert_ids[None], gate_weights[None],
         queries, resid, w_in, w_out,
     )
-    hidden, outgoing = attend([*blocks, keys], [*blocks, values], queries, resid, norm_gain[None], bias, placing)
+    weights, totals = weigh([*key_blocks, keys], queries, bias)
+    hidden, outgoing = mix([*value_blocks, values], weights, totals, resid, norm_gain[None], placing)
 
     def exchange(block):
         return lax.all_to_all(

time: 83.3 us -> 78.8 us (0.946)
  blocking collectives: 62.8 us -> 60 us
  local copies, waits for them, and re-layouts: 1.76 us -> 0.01 us
  starting transfers between devices: 8.24 us -> 6.69 us
  waiting for transfers between devices: 0.01 us -> 1.33 us
    all_to_all x2, blocking collectives: 62.8 us -> 60 us  [exchange(): lax.all_to_all(block.reshape(devices, capacity, model_width), ('exp', 'se...]
    ppermute x2 -> x4, starting transfers between devices: 8.24 us -> 6.69 us  [earlier(): lax.ppermute(own, 'seq', [(i, (i + hop) % seq_count) for i in range(seq_c...]
    ppermute x2 -> x4, waiting for transfers between devices: 0.01 us -> 1.33 us  [earlier(): lax.ppermute(own, 'seq', [(i, (i + hop) % seq_count) for i in range(seq_c...]
    unnamed x7 -> x6, local copies, waits for them, and re-layouts: 0.92 us -> 0.01 us
    concatenate x1 -> x0, local copies, waits for them, and re-layouts: 0.84 us -> none  [per_device(): own = jnp.concatenate([keys, values], axis=1)]
    pallas_call x1 -> x2, Pallas kernels: 2.23 us -> 2.59 us  [the longest x1 1.32 us: mix(): pl.pallas_call(functools.partial(mix_kernel, len(values)), out_shape=(plt...]
  transfers between devices with their start and end apart: 2 -> 4, of which waited for: 0 -> 1; matrix products, arithmetic and copies ran while one was open for 0% -> 0% of each run, Pallas kernels for 5% -> 7%
where the time goes in v3:
time: 78.8 us; the launch traced here: 78.6 us
  blocking collectives  60 us (76%)
  Pallas kernels  10.5 us (13%)
  starting transfers between devices  6.69 us (8%)
  waiting for transfers between devices  1.33 us (2%)
    all_to_all x2, blocking collectives, exchange(): lax.all_to_all(block.reshape(devices, capacity, model_width), ('exp', 'se...  60 us
    ppermute x4, starting transfers between devices, earlier(): lax.ppermute(own, 'seq', [(i, (i + hop) % seq_count) for i in range(seq_c...  6.69 us
    pallas_call x1, Pallas kernels, stage(): pl.pallas_call(functools.partial(stage_kernel, before, splits, capacity),...  4.15 us
    pallas_call x1, Pallas kernels, experts(): pl.pallas_call(expert_kernel, out_shape=jax.ShapeDtypeStruct((rows, model...  2.61 us
  transfers between devices with their start and end apart: 4, of which 1 were waited for; matrix products, arithmetic and copies ran while one was open for 0% of the time, Pallas kernels for 7%

profile of v3, /device:TPU:1, one launch (start us, length us, event | category | flops | bytes accessed | tf_op | source)
XLA Modules:
  0.0 78.6 jit_solution(14574925524855642489)
XLA Ops:
  0.0 3.1 %collective-permute-start.2 = (bf16[128,256]{1,0:T(8,128)(2,1)}, bf16[128,256]{1,0:T(8,128)(2,1)S(1)}, u32[]{:S(2)}, u32[]{:S(2)}) collective-permute-start(bf16[128,256]{1,0:T(8,128)(2,1)} %refs_2_.2), channel_id=1, source_target_pairs={{0,2},{1,3},{2,0},{3,1},{4,6},{5,7},{6,4},{7,5},{8,10},{9,11},{10,... | collective-permute-start | bytes 196616 | tf_op jit(solution)/shard_map/ppermute | solution.py:298
  3.1 1.3 %collective-permute-start.3 = (bf16[128,256]{1,0:T(8,128)(2,1)}, bf16[128,256]{1,0:T(8,128)(2,1)S(1)}, u32[]{:S(2)}, u32[]{:S(2)}) collective-permute-start(bf16[128,256]{1,0:T(8,128)(2,1)} %refs_2_.2), channel_id=1, source_target_pairs={{0,1},{1,2},{2,3},{3,0},{4,5},{5,6},{6,7},{7,4},{8,9},{9,10},{10,1... | collective-permute-start | bytes 196616 | tf_op jit(solution)/shard_map/ppermute | solution.py:298
  4.4 0.1 collective-permute-start
  4.5 2.2 %collective-permute-start.1 = (bf16[128,256]{1,0:T(8,128)(2,1)}, bf16[128,256]{1,0:T(8,128)(2,1)S(1)}, u32[]{:S(2)}, u32[]{:S(2)}) collective-permute-start(bf16[128,256]{1,0:T(8,128)(2,1)} %refs_2_.3), channel_id=1, source_target_pairs={{0,1},{1,2},{2,3},{3,0},{4,5},{5,6},{6,7},{7,4},{8,9},{9,10},{10,1... | collective-permute-start | bytes 196616 | tf_op jit(solution)/shard_map/ppermute | solution.py:298
  6.7 0.0 copy-start.2
  6.7 0.0 copy-start
  6.7 0.0 copy-start.1
  6.7 4.1 %stage.1 = (bf16[128,2048]{1,0:T(8,128)(2,1)S(1)}, bf16[128,2048]{1,0:T(8,128)(2,1)S(1)}, bf16[1,2048,1536]{2,1,0:T(8,128)(2,1)S(1)}, bf16[1,768,2048]{2,1,0:T(8...) custom-call(s32[1,512]{1,0:T(1,128)} %bitcast.13, ...), custom_call_target="tpu_custom_call" | custom-call | bytes 10485760 | tf_op jit(solution)/shard_map/stage/pallas_call | solution.py:88
  10.8 0.0 collective-permute-done.2.refs_0_
  10.9 0.0 collective-permute-done.3.refs_1_
  10.9 0.0 copy-done.2
  10.9 1.3 %weigh.1 = (bf16[8,384,256]{2,1,0:T(8,128)(2,1)S(1)}, f32[8,256]{1,0:T(8,128)S(1)}) custom-call(bf16[128,256]{1,0:T(8,128)(2,1)S(1)} %collective-permute-done.2.refs_0_, bf16[128,256]{1,0:T(8,128)(2,1)S(1)} %collective-permute-done.3.refs_1_, bf16[128,256]{1,0:T(8,128)(2,1)S(1)} %copy-done.2, bf16[128,2048]{1,0:T(8,128)(2,1)S(1)} %get-tuple-element.17.refs_3_, ...), custom_call_target="tpu_custom_call" | custom-call | flops 402653184 | bytes 1048576 | tf_op jit(solution)/shard_map/weigh/pallas_call | solution.py:149
  12.1 1.3 %collective-permute-done.refs_0_ = bf16[128,256]{1,0:T(8,128)(2,1)S(1)} collective-permute-done((bf16[128,256]{1,0:T(8,128)(2,1)}, bf16[128,256]{1,0:T(8,128)(2,1)S(1)}, u32[]{:S(2)}, u32[]{:S(2)}) %collective-permute-start) | collective-permute-done | bytes 65568 | tf_op jit(solution)/shard_map/ppermute | solution.py:298
  13.5 0.0 collective-permute-done.1.refs_1_
  13.5 0.0 copy-done
  13.5 0.0 copy-done.1
  13.5 1.3 %mix.1 = (bf16[128,2048]{1,0:T(8,128)(2,1)S(1)}, bf16[256,2048]{1,0:T(8,128)(2,1)S(1)}) custom-call(bf16[128,256]{1,0:T(8,128)(2,1)S(1)} %collective-permute-done.refs_0_, bf16[128,256]{1,0:T(8,128)(2,1)S(1)} %collective-permute-done.1.refs_1_, bf16[128,256]{1,0:T(8,128)(2,1)S(1)} %copy-done, bf16[8,384,256]{2,1,0:T(8,128)(2,1)S(1)} %get-tuple-element.19.refs_3_, ...), custom_call_target="tpu_custom_call" | custom-call | tf_op jit(solution)/shard_map/mix/pallas_call | solution.py:210
  14.8 30.7 %all_to_all.10 = bf16[32,8,2048]{2,1,0:T(8,128)(2,1)S(1)} all-to-all(bf16[32,8,2048]{2,1,0:T(8,128)(2,1)S(1)} %bitcast.11), channel_id=1, replica_groups=mesh['exp'=8,'seq'=4] {'exp','seq'}, dimensions={0} | all-to-all | bytes 2097152 | tf_op jit(solution)/shard_map/all_to_all | solution.py:311
  45.5 2.6 %experts.1 = bf16[256,2048]{1,0:T(8,128)(2,1)S(1)} custom-call(bf16[256,2048]{1,0:T(8,128)(2,1)S(1)} %bitcast.9, bf16[1,2048,1536]{2,1,0:T(8,128)(2,1)S(1)} %get-tuple-element.24.in_ref, bf16[1,768,2048]{2,1,0:T(8,128)(2,1)S(1)} %get-tuple-element.25.down_ref), custom_call_target="tpu_custom_call" | custom-call | tf_op jit(solution)/shard_map/experts/pallas_call | solution.py:249
  48.1 29.3 %all_to_all.11 = bf16[32,8,2048]{2,1,0:T(8,128)(2,1)S(1)} all-to-all(bf16[32,8,2048]{2,1,0:T(8,128)(2,1)S(1)} %bitcast.10), channel_id=1, replica_groups=mesh['exp'=8,'seq'=4] {'exp','seq'}, dimensions={0} | all-to-all | bytes 2097152 | tf_op jit(solution)/shard_map/all_to_all | solution.py:311
  77.5 1.1 %combine.1 = bf16[128,2048]{1,0:T(8,128)(2,1)} custom-call(bf16[256,2048]{1,0:T(8,128)(2,1)S(1)} %bitcast.8, bf16[128,2048]{1,0:T(8,128)(2,1)S(1)} %get-tuple-element.26.hidden_ref, bf16[128,256]{1,0:T(8,128)(2,1)S(1)} %get-tuple-element.27.picking_ref, f32[128,128]{1,0:T(8,128)S(1)} %get-tuple-element.28.gates_ref), custom_call_target="tpu_custom_call" | custom-call | tf_op jit(solution)/shard_map/combine/pallas_call | solution.py:271
Async XLA Ops:
  0.0 10.8 %collective-permute-start.2 = (bf16[128,256]{1,0:T(8,128)(2,1)}, bf16[128,256]{1,0:T(8,128)(2,1)S(1)}, u32[]{:S(2)}, u32[]{:S(2)}) collective-permute-start(bf16[128,256]{1,0:T(8,128)(2,1)} %refs_2_.2), channel_id=1, source_target_pairs={{0,2},{1,3},{2,0},{3,1},{4,6},{5,7},{6,4},{7,5},{8,10},{9,11},{10,... | collective-permute-start | bytes 196616 | tf_op jit(solution)/shard_map/ppermute | solution.py:298
  3.1 7.7 %collective-permute-start.3 = (bf16[128,256]{1,0:T(8,128)(2,1)}, bf16[128,256]{1,0:T(8,128)(2,1)S(1)}, u32[]{:S(2)}, u32[]{:S(2)}) collective-permute-start(bf16[128,256]{1,0:T(8,128)(2,1)} %refs_2_.2), channel_id=1, source_target_pairs={{0,1},{1,2},{2,3},{3,0},{4,5},{5,6},{6,7},{7,4},{8,9},{9,10},{10,1... | collective-permute-start | bytes 196616 | tf_op jit(solution)/shard_map/ppermute | solution.py:298
  4.4 9.0 %collective-permute-start = (bf16[128,256]{1,0:T(8,128)(2,1)}, bf16[128,256]{1,0:T(8,128)(2,1)S(1)}, u32[]{:S(2)}, u32[]{:S(2)}) collective-permute-start(bf16[128,256]{1,0:T(8,128)(2,1)} %refs_2_.3), channel_id=1, source_target_pairs={{0,2},{1,3},{2,0},{3,1},{4,6},{5,7},{6,4},{7,5},{8,10},{9,11},{10,... | collective-permute-start | bytes 196616 | tf_op jit(solution)/shard_map/ppermute | solution.py:298
  4.5 9.0 %collective-permute-start.1 = (bf16[128,256]{1,0:T(8,128)(2,1)}, bf16[128,256]{1,0:T(8,128)(2,1)S(1)}, u32[]{:S(2)}, u32[]{:S(2)}) collective-permute-start(bf16[128,256]{1,0:T(8,128)(2,1)} %refs_2_.3), channel_id=1, source_target_pairs={{0,1},{1,2},{2,3},{3,0},{4,5},{5,6},{6,7},{7,4},{8,9},{9,10},{10,1... | collective-permute-start | bytes 196616 | tf_op jit(solution)/shard_map/ppermute | solution.py:298
  6.7 4.2 %copy-start.2 = (bf16[128,256]{1,0:T(8,128)(2,1)S(1)}, bf16[128,256]{1,0:T(8,128)(2,1)}, u32[]{:S(2)}) copy-start(bf16[128,256]{1,0:T(8,128)(2,1)} %refs_2_.2) | copy-start | bytes 196612
  6.7 6.8 %copy-start = (bf16[128,256]{1,0:T(8,128)(2,1)S(1)}, bf16[128,256]{1,0:T(8,128)(2,1)}, u32[]{:S(2)}) copy-start(bf16[128,256]{1,0:T(8,128)(2,1)} %refs_2_.3) | copy-start | bytes 196612
  6.7 6.8 %copy-start.1 = (f32[2048]{0:T(1024)S(1)}, f32[2048]{0:T(1024)}, u32[]{:S(2)}) copy-start(f32[2048]{0:T(1024)} %param.15) | copy-start | bytes 24580

commit v4 on v3

--- a/solution.py
+++ b/solution.py
@@ -21,6 +21,7 @@
 SCALE = 1.0 / math.sqrt(HD)
 GROUP = HEADS // KVH
 MIB = 2**20
+STAGED = 9
 PAIRS = HEADS // 2
 BY_ROWS = (((1,), (1,)), ((), ()))
 
@@ -43,16 +44,28 @@
     return jnp.sum(kept, axis=1, keepdims=True)
 
 
+def pieces(source, target):
+    axis, count = source.ndim - 2, source.shape[-2]
+    parts = max(1, source.size // MIB)
+    while count % (16 * parts):
+        parts -= 1
+    step = count // parts
+    for low in range(0, count, step):
+        at = (0,) * axis + (slice(low, low + step),)
+        yield source.at[at], target.at[at]
+
+
 def stage_kernel(before, splits, capacity, *refs):
-    count = 7
+    count = STAGED
     sources, refs = refs[:count], refs[count:]
     copied, refs = refs[: count - 3], refs[count - 3 :]
     bias_ref, placing_ref, picking_ref, gates_ref, refs = *refs[:4], refs[4:]
     small, sems = refs[:3], refs[3]
-    copies = [
-        pltpu.make_async_copy(source, target, sems.at[i])
-        for i, (source, target) in enumerate(zip(sources, (*small, *copied)))
-    ]
+    copies = []
+    for source, target in zip(sources, (*small, *copied)):
+        whole = source.shape[-2] % 16 != 0
+        for part, place_for in [(source, target)] if whole else pieces(source, target):
+            copies.append(pltpu.make_async_copy(part, place_for, sems.at[len(copies)]))
     for copy in copies:
         copy.start()
     seg_ref, ids_ref, gate_row_ref = small
@@ -98,7 +111,7 @@
         out_specs=(VMEM,) * (len(large) + 4),
         scratch_shapes=[
             *[pltpu.VMEM(array.shape, array.dtype) for array in (seg, ids, gates)],
-            pltpu.SemaphoreType.DMA((len(sources),)),
+            pltpu.SemaphoreType.DMA((32,)),
         ],
         compiler_params=pltpu.CompilerParams(vmem_limit_bytes=16 * MIB),
         cost_estimate=pl.CostEstimate(flops=0, bytes_accessed=10 * MIB, transcendentals=0),
@@ -257,22 +270,34 @@
     )(rows_in, w_in, w_out)
 
 
-def combine_kernel(delivered_ref, hidden_ref, picking_ref, gates_ref, out_ref):
+def combine_kernel(delivered_ref, hidden_ref, picking_ref, gates_ref, out_ref, made_ref, sems):
     step = 512
     gates = jnp.concatenate([gates_ref[...]] * (step // gates_ref.shape[1]), 1)
+    picking = picking_ref[...]
+    copies = []
     for low in range(0, hidden_ref.shape[1], step):
         cols = slice(low, low + step)
-        routed = jnp.dot(picking_ref[...], delivered_ref[:, cols], preferred_element_type=F32)
+        routed = jnp.dot(picking, delivered_ref[:, cols], preferred_element_type=F32)
         routed = routed.astype(BF16).astype(F32)
-        out_ref[:, cols] = (hidden_ref[:, cols].astype(F32) + gates * routed).astype(BF16)
+        made_ref[:, cols] = (hidden_ref[:, cols].astype(F32) + gates * routed).astype(BF16)
+        copies.append(
+            pltpu.make_async_copy(made_ref.at[:, cols], out_ref.at[:, cols], sems.at[low // step])
+        )
+        copies[-1].start()
+    for copy in copies:
+        copy.wait()
 
 
 def combine(delivered, hidden, picking, gates):
     return pl.pallas_call(
         combine_kernel,
-        out_shape=jax.ShapeDtypeStruct(hidden.shape, BF16),
+        out_shape=pltpu.HBM(hidden.shape, BF16),
         in_specs=[VMEM] * 4,
-        out_specs=VMEM,
+        out_specs=HBM,
+        scratch_shapes=[
+            pltpu.VMEM(hidden.shape, BF16),
+            pltpu.SemaphoreType.DMA((hidden.shape[1] // 512,)),
+        ],
         compiler_params=pltpu.CompilerParams(vmem_limit_bytes=16 * MIB),
         name="combine",
     )(delivered, hidden, picking, gates)
@@ -295,17 +320,17 @@
 
     def earlier(own):
         return [
-            lax.ppermute(own, "seq", [(i, (i + hop) % seq_count) for i in range(seq_count)])
+            lax.ppermute(own, "seq", [(i, (i + hop) % seq_count if i + hop < seq_count else (seq_count - 1 - i) if hop == 2 else (i + hop) % seq_count) for i in range(seq_count)])
             for hop in range(before, 0, -1)
         ]
 
     key_blocks, value_blocks = earlier(keys), earlier(values)
-    queries, resid, w_in, w_out, bias, placing, picking, gates = stage(
+    queries, keys, values, resid, gain, w_in, bias, placing, picking, gates = stage(
         before, splits, capacity, slots, seg_ids[None], expert_ids[None], gate_weights[None],
-        queries, resid, w_in, w_out,
+        queries, keys, values, resid, norm_gain[None], w_in,
     )
     weights, totals = weigh([*key_blocks, keys], queries, bias)
-    hidden, outgoing = mix([*value_blocks, values], weights, totals, resid, norm_gain[None], placing)
+    hidden, outgoing = mix([*value_blocks, values], weights, totals, resid, gain, placing)
 
     def exchange(block):
         return lax.all_to_all(

time: 78.8 us -> 78.3 us (level)
  blocking collectives: 60 us -> 62.5 us
  waiting for transfers between devices: 1.33 us -> 0.01 us
  starting transfers between devices: 6.69 us -> 5.67 us
    all_to_all x2, blocking collectives: 60 us -> 62.5 us  [exchange(): lax.all_to_all(block.reshape(devices, capacity, model_width), ('exp', 'se...]
    ppermute x4, waiting for transfers between devices: 1.33 us -> 0.01 us  [earlier(): lax.ppermute(own, 'seq', [(i, (i + hop) % seq_count if i + hop < seq_coun...]
    ppermute x4, starting transfers between devices: 6.69 us -> 5.67 us  [earlier(): lax.ppermute(own, 'seq', [(i, (i + hop) % seq_count if i + hop < seq_coun...]
  transfers between devices with their start and end apart: 4 -> 4, of which waited for: 1 -> 0; matrix products, arithmetic and copies ran while one was open for 0% -> 0% of each run, Pallas kernels for 7% -> 6%
where the time goes in v4:
time: 78.3 us; the launch traced here: 78.1 us
  blocking collectives  62.5 us (80%)
  Pallas kernels  9.9 us (13%)
  starting transfers between devices  5.67 us (7%)
    all_to_all x2, blocking collectives, exchange(): lax.all_to_all(block.reshape(devices, capacity, model_width), ('exp', 'se...  62.5 us
    ppermute x4, starting transfers between devices, earlier(): lax.ppermute(own, 'seq', [(i, (i + hop) % seq_count if i + hop < seq_coun...  5.67 us
    pallas_call x1, Pallas kernels, stage(): pl.pallas_call(functools.partial(stage_kernel, before, splits, capacity),...  3.67 us
    pallas_call x1, Pallas kernels, experts(): pl.pallas_call(expert_kernel, out_shape=jax.ShapeDtypeStruct((rows, model...  2.61 us
  transfers between devices with their start and end apart: 4, of which 0 were waited for; matrix products, arithmetic and copies ran while one was open for 0% of the time, Pallas kernels for 6%

profile of v4, /device:TPU:1, one launch (start us, length us, event | category | flops | bytes accessed | tf_op | source)
XLA Modules:
  0.0 78.1 jit_solution(4402171773229162596)
XLA Ops:
  0.0 2.1 %collective-permute-start.3 = (bf16[128,256]{1,0:T(8,128)(2,1)}, bf16[128,256]{1,0:T(8,128)(2,1)S(1)}, u32[]{:S(2)}, u32[]{:S(2)}) collective-permute-start(bf16[128,256]{1,0:T(8,128)(2,1)} %refs_4_.1), channel_id=1, source_target_pairs={{0,1},{1,2},{2,3},{3,0},{4,5},{5,6},{6,7},{7,4},{8,9},{9,10},{10,1... | collective-permute-start | bytes 196616 | tf_op jit(solution)/shard_map/ppermute | solution.py:323
  2.1 2.3 %collective-permute-start.2 = (bf16[128,256]{1,0:T(8,128)(2,1)}, bf16[128,256]{1,0:T(8,128)(2,1)S(1)}, u32[]{:S(2)}, u32[]{:S(2)}) collective-permute-start(bf16[128,256]{1,0:T(8,128)(2,1)} %refs_4_.1), channel_id=1, source_target_pairs={{0,2},{1,3},{2,1},{3,0},{4,6},{5,7},{6,5},{7,4},{8,10},{9,11},{10,... | collective-permute-start | bytes 196616 | tf_op jit(solution)/shard_map/ppermute | solution.py:323
  4.4 0.2 collective-permute-start
  4.6 1.1 %collective-permute-start.1 = (bf16[128,256]{1,0:T(8,128)(2,1)}, bf16[128,256]{1,0:T(8,128)(2,1)S(1)}, u32[]{:S(2)}, u32[]{:S(2)}) collective-permute-start(bf16[128,256]{1,0:T(8,128)(2,1)} %refs_5_.1), channel_id=1, source_target_pairs={{0,1},{1,2},{2,3},{3,0},{4,5},{5,6},{6,7},{7,4},{8,9},{9,10},{10,1... | collective-permute-start | bytes 196616 | tf_op jit(solution)/shard_map/ppermute | solution.py:323
  5.7 0.0 copy-start
  5.7 3.7 %stage.1 = (bf16[128,2048]{1,0:T(8,128)(2,1)S(1)}, bf16[128,256]{1,0:T(8,128)(2,1)S(1)}, bf16[128,256]{1,0:T(8,128)(2,1)S(1)}, bf16[128,2048]{1,0:T(8,128)(2,1)S...) custom-call(s32[1,512]{1,0:T(1,128)} %bitcast.13, ...), custom_call_target="tpu_custom_call" | custom-call | bytes 10485760 | tf_op jit(solution)/shard_map/stage/pallas_call | solution.py:101
  9.4 0.0 collective-permute-done.3.refs_1_
  9.4 0.0 collective-permute-done.2.refs_0_
  9.4 1.3 %weigh.1 = (bf16[8,384,256]{2,1,0:T(8,128)(2,1)S(1)}, f32[8,256]{1,0:T(8,128)S(1)}) custom-call(bf16[128,256]{1,0:T(8,128)(2,1)S(1)} %collective-permute-done.2.refs_0_, bf16[128,256]{1,0:T(8,128)(2,1)S(1)} %collective-permute-done.3.refs_1_, bf16[128,256]{1,0:T(8,128)(2,1)S(1)} %get-tuple-element.20.refs_2_, ...), custom_call_target="tpu_custom_call" | custom-call | flops 402653184 | bytes 1048576 | tf_op jit(solution)/shard_map/weigh/pallas_call | solution.py:162
  10.7 0.0 collective-permute-done.refs_0_
  10.7 0.0 collective-permute-done.1.refs_1_
  10.7 1.3 %mix.1 = (bf16[128,2048]{1,0:T(8,128)(2,1)S(1)}, bf16[256,2048]{1,0:T(8,128)(2,1)S(1)}) custom-call(bf16[128,256]{1,0:T(8,128)(2,1)S(1)} %collective-permute-done.refs_0_, bf16[128,256]{1,0:T(8,128)(2,1)S(1)} %collective-permute-done.1.refs_1_, bf16[128,256]{1,0:T(8,128)(2,1)S(1)} %get-tuple-element.19.refs_2_, ...), custom_call_target="tpu_custom_call" | custom-call | tf_op jit(solution)/shard_map/mix/pallas_call | solution.py:223
  12.0 33.2 %all_to_all.10 = bf16[32,8,2048]{2,1,0:T(8,128)(2,1)S(1)} all-to-all(bf16[32,8,2048]{2,1,0:T(8,128)(2,1)S(1)} %bitcast.11), channel_id=1, replica_groups=mesh['exp'=8,'seq'=4] {'exp','seq'}, dimensions={0} | all-to-all | bytes 2097152 | tf_op jit(solution)/shard_map/all_to_all | solution.py:336
  45.1 0.0 copy-done
  45.1 2.6 %experts.1 = bf16[256,2048]{1,0:T(8,128)(2,1)S(1)} custom-call(bf16[256,2048]{1,0:T(8,128)(2,1)S(1)} %bitcast.9, bf16[1,2048,1536]{2,1,0:T(8,128)(2,1)S(1)} %get-tuple-element.29.in_ref, bf16[1,768,2048]{2,1,0:T(8,128)(2,1)S(1)} %copy-done), custom_call_target="tpu_custom_call" | custom-call | tf_op jit(solution)/shard_map/experts/pallas_call | solution.py:262
  47.8 29.3 %all_to_all.11 = bf16[32,8,2048]{2,1,0:T(8,128)(2,1)S(1)} all-to-all(bf16[32,8,2048]{2,1,0:T(8,128)(2,1)S(1)} %bitcast.10), channel_id=1, replica_groups=mesh['exp'=8,'seq'=4] {'exp','seq'}, dimensions={0} | all-to-all | bytes 2097152 | tf_op jit(solution)/shard_map/all_to_all | solution.py:336
  77.1 1.0 %combine.1 = bf16[128,2048]{1,0:T(8,128)(2,1)} custom-call(bf16[256,2048]{1,0:T(8,128)(2,1)S(1)} %bitcast.8, bf16[128,2048]{1,0:T(8,128)(2,1)S(1)} %get-tuple-element.30.hidden_ref, bf16[128,256]{1,0:T(8,128)(2,1)S(1)} %get-tuple-element.31.picking_ref, f32[128,128]{1,0:T(8,128)S(1)} %get-tuple-element.32.gates_ref), custom_call_target="tpu_custom_call" | custom-call | tf_op jit(solution)/shard_map/combine/pallas_call | solution.py:292
Async XLA Ops:
  0.0 9.4 %collective-permute-start.3 = (bf16[128,256]{1,0:T(8,128)(2,1)}, bf16[128,256]{1,0:T(8,128)(2,1)S(1)}, u32[]{:S(2)}, u32[]{:S(2)}) collective-permute-start(bf16[128,256]{1,0:T(8,128)(2,1)} %refs_4_.1), channel_id=1, source_target_pairs={{0,1},{1,2},{2,3},{3,0},{4,5},{5,6},{6,7},{7,4},{8,9},{9,10},{10,1... | collective-permute-start | bytes 196616 | tf_op jit(solution)/shard_map/ppermute | solution.py:323
  2.1 7.2 %collective-permute-start.2 = (bf16[128,256]{1,0:T(8,128)(2,1)}, bf16[128,256]{1,0:T(8,128)(2,1)S(1)}, u32[]{:S(2)}, u32[]{:S(2)}) collective-permute-start(bf16[128,256]{1,0:T(8,128)(2,1)} %refs_4_.1), channel_id=1, source_target_pairs={{0,2},{1,3},{2,1},{3,0},{4,6},{5,7},{6,5},{7,4},{8,10},{9,11},{10,... | collective-permute-start | bytes 196616 | tf_op jit(solution)/shard_map/ppermute | solution.py:323
  4.4 6.2 %collective-permute-start = (bf16[128,256]{1,0:T(8,128)(2,1)}, bf16[128,256]{1,0:T(8,128)(2,1)S(1)}, u32[]{:S(2)}, u32[]{:S(2)}) collective-permute-start(bf16[128,256]{1,0:T(8,128)(2,1)} %refs_5_.1), channel_id=1, source_target_pairs={{0,2},{1,3},{2,1},{3,0},{4,6},{5,7},{6,5},{7,4},{8,10},{9,11},{10,... | collective-permute-start | bytes 196616 | tf_op jit(solution)/shard_map/ppermute | solution.py:323
  4.6 6.1 %collective-permute-start.1 = (bf16[128,256]{1,0:T(8,128)(2,1)}, bf16[128,256]{1,0:T(8,128)(2,1)S(1)}, u32[]{:S(2)}, u32[]{:S(2)}) collective-permute-start(bf16[128,256]{1,0:T(8,128)(2,1)} %refs_5_.1), channel_id=1, source_target_pairs={{0,1},{1,2},{2,3},{3,0},{4,5},{5,6},{6,7},{7,4},{8,9},{9,10},{10,1... | collective-permute-start | bytes 196616 | tf_op jit(solution)/shard_map/ppermute | solution.py:323
  5.7 39.5 %copy-start = (bf16[1,768,2048]{2,1,0:T(8,128)(2,1)S(1)}, bf16[1,768,2048]{2,1,0:T(8,128)(2,1)}, u32[]{:S(2)}) copy-start(bf16[1,768,2048]{2,1,0:T(8,128)(2,1)} %down_ref.1) | copy-start | bytes 9437188

commit v5 on v4

--- a/solution.py
+++ b/solution.py
@@ -86,10 +86,10 @@
         bias_ref[block * rows : (block + 1) * rows, :] = jnp.where(allowed, 0.0, -jnp.inf)
     slots = placing_ref.shape[0]
     ids_row = ids_ref[...]
-    first = slots_of(ids_row, splits, capacity, 1)
-    placing_ref[...] = one_hot(first, iota((slots, rows), 0), splits, capacity)
-    first = slots_of(ids_row, splits, capacity, 0)
-    picking_ref[...] = one_hot(first, iota((rows, slots), 1), splits, capacity)
+    token_slots = slots_of(ids_row, splits, capacity, 1)
+    placing_ref[...] = one_hot(token_slots, iota((slots, rows), 0))
+    token_slots = slots_of(ids_row, splits, capacity, 0)
+    picking_ref[...] = one_hot(token_slots, iota((rows, slots), 1))
     gates_ref[...] = jnp.broadcast_to(as_column(gate_row_ref[...]), gates_ref.shape)
     for copy in copies[3:]:
         copy.wait()
@@ -119,19 +119,26 @@
     )(*[pltpu.with_memory_space_constraint(array, pltpu.HBM) for array in sources])
 
 
+def place_of(device, seq_count):
+    low = device & (seq_count - 1)
+    return device - low + ((seq_count - low) & (seq_count - 1))
+
+
 def slots_of(ids_row, splits, capacity, axis):
     count = ids_row.shape[1]
     ids_col = as_column(ids_row)
     earlier = iota((count, count), 1 - axis) < iota((count, count), axis)
     same = ((ids_col == ids_row) & earlier).astype(F32)
     rank = jnp.sum(same, axis=1 - axis, keepdims=True).astype(jnp.int32)
-    return (ids_row if axis == 1 else ids_col) * (splits * capacity) + rank
-
-
-def one_hot(first, slot_at, splits, capacity):
-    hot = slot_at == first
-    for split in range(1, splits):
-        hot = hot | (slot_at == first + split * capacity)
+    first = (ids_row if axis == 1 else ids_col) * splits
+    seq_count = lax.axis_size("seq")
+    return [place_of(first + split, seq_count) * capacity + rank for split in range(splits)]
+
+
+def one_hot(slots, slot_at):
+    hot = slot_at == slots[0]
+    for slot in slots[1:]:
+        hot = hot | (slot_at == slot)
     return hot.astype(F32).astype(BF16)
 
 
@@ -339,6 +346,7 @@
             split_axis=0,
             concat_axis=0,
             tiled=True,
+            axis_index_groups=[[place_of(device, seq_count) for device in range(devices)]],
         ).reshape(slots, model_width)
 
     delivered = exchange(experts(exchange(outgoing), w_in, w_out))

time: 78.3 us -> 77.8 us (level)
  no operation moved by 1% of the time
where the time goes in v5:
time: 77.8 us; the launch traced here: 77.6 us
  blocking collectives  61.9 us (80%)
  Pallas kernels  9.9 us (13%)
  starting transfers between devices  5.67 us (7%)
    all_to_all x2, blocking collectives, exchange(): lax.all_to_all(block.reshape(devices, capacity, model_width), ('exp', 'se...  61.9 us
    ppermute x4, starting transfers between devices, earlier(): lax.ppermute(own, 'seq', [(i, (i + hop) % seq_count if i + hop < seq_coun...  5.67 us
    pallas_call x1, Pallas kernels, stage(): pl.pallas_call(functools.partial(stage_kernel, before, splits, capacity),...  3.67 us
    pallas_call x1, Pallas kernels, experts(): pl.pallas_call(expert_kernel, out_shape=jax.ShapeDtypeStruct((rows, model...  2.61 us
  transfers between devices with their start and end apart: 4, of which 0 were waited for; matrix products, arithmetic and copies ran while one was open for 0% of the time, Pallas kernels for 6%

profile of v5, /device:TPU:1, one launch (start us, length us, event | category | flops | bytes accessed | tf_op | source)
XLA Modules:
  0.0 77.6 jit_solution(10315534769021043622)
XLA Ops:
  0.0 2.1 %collective-permute-start.3 = (bf16[128,256]{1,0:T(8,128)(2,1)}, bf16[128,256]{1,0:T(8,128)(2,1)S(1)}, u32[]{:S(2)}, u32[]{:S(2)}) collective-permute-start(bf16[128,256]{1,0:T(8,128)(2,1)} %refs_4_.1), channel_id=1, source_target_pairs={{0,1},{1,2},{2,3},{3,0},{4,5},{5,6},{6,7},{7,4},{8,9},{9,10},{10,1... | collective-permute-start | bytes 196616 | tf_op jit(solution)/shard_map/ppermute | solution.py:330
  2.1 2.3 %collective-permute-start.2 = (bf16[128,256]{1,0:T(8,128)(2,1)}, bf16[128,256]{1,0:T(8,128)(2,1)S(1)}, u32[]{:S(2)}, u32[]{:S(2)}) collective-permute-start(bf16[128,256]{1,0:T(8,128)(2,1)} %refs_4_.1), channel_id=1, source_target_pairs={{0,2},{1,3},{2,1},{3,0},{4,6},{5,7},{6,5},{7,4},{8,10},{9,11},{10,... | collective-permute-start | bytes 196616 | tf_op jit(solution)/shard_map/ppermute | solution.py:330
  4.4 0.2 collective-permute-start
  4.6 1.1 %collective-permute-start.1 = (bf16[128,256]{1,0:T(8,128)(2,1)}, bf16[128,256]{1,0:T(8,128)(2,1)S(1)}, u32[]{:S(2)}, u32[]{:S(2)}) collective-permute-start(bf16[128,256]{1,0:T(8,128)(2,1)} %refs_5_.1), channel_id=1, source_target_pairs={{0,1},{1,2},{2,3},{3,0},{4,5},{5,6},{6,7},{7,4},{8,9},{9,10},{10,1... | collective-permute-start | bytes 196616 | tf_op jit(solution)/shard_map/ppermute | solution.py:330
  5.7 0.0 copy-start
  5.7 3.7 %stage.1 = (bf16[128,2048]{1,0:T(8,128)(2,1)S(1)}, bf16[128,256]{1,0:T(8,128)(2,1)S(1)}, bf16[128,256]{1,0:T(8,128)(2,1)S(1)}, bf16[128,2048]{1,0:T(8,128)(2,1)S...) custom-call(s32[1,512]{1,0:T(1,128)} %bitcast.13, ...), custom_call_target="tpu_custom_call" | custom-call | bytes 10485760 | tf_op jit(solution)/shard_map/stage/pallas_call | solution.py:101
  9.4 0.0 collective-permute-done.3.refs_1_
  9.4 0.0 collective-permute-done.2.refs_0_
  9.4 1.3 %weigh.1 = (bf16[8,384,256]{2,1,0:T(8,128)(2,1)S(1)}, f32[8,256]{1,0:T(8,128)S(1)}) custom-call(bf16[128,256]{1,0:T(8,128)(2,1)S(1)} %collective-permute-done.2.refs_0_, bf16[128,256]{1,0:T(8,128)(2,1)S(1)} %collective-permute-done.3.refs_1_, bf16[128,256]{1,0:T(8,128)(2,1)S(1)} %get-tuple-element.20.refs_2_, ...), custom_call_target="tpu_custom_call" | custom-call | flops 402653184 | bytes 1048576 | tf_op jit(solution)/shard_map/weigh/pallas_call | solution.py:169
  10.7 0.0 collective-permute-done.refs_0_
  10.7 0.0 collective-permute-done.1.refs_1_
  10.7 1.3 %mix.1 = (bf16[128,2048]{1,0:T(8,128)(2,1)S(1)}, bf16[256,2048]{1,0:T(8,128)(2,1)S(1)}) custom-call(bf16[128,256]{1,0:T(8,128)(2,1)S(1)} %collective-permute-done.refs_0_, bf16[128,256]{1,0:T(8,128)(2,1)S(1)} %collective-permute-done.1.refs_1_, bf16[128,256]{1,0:T(8,128)(2,1)S(1)} %get-tuple-element.19.refs_2_, ...), custom_call_target="tpu_custom_call" | custom-call | tf_op jit(solution)/shard_map/mix/pallas_call | solution.py:230
  12.0 33.2 %all_to_all.10 = bf16[32,8,2048]{2,1,0:T(8,128)(2,1)S(1)} all-to-all(bf16[32,8,2048]{2,1,0:T(8,128)(2,1)S(1)} %bitcast.11), channel_id=1, replica_groups={{0,3,2,1,4,7,6,5,8,11,10,9,12,15,14,13,16,19,18,17,20,23,22,21,24,27,26..., dimensions={0} | all-to-all | bytes 2097152 | tf_op jit(solution)/shard_map/all_to_all | solution.py:343
  45.1 0.0 copy-done
  45.1 2.6 %experts.1 = bf16[256,2048]{1,0:T(8,128)(2,1)S(1)} custom-call(bf16[256,2048]{1,0:T(8,128)(2,1)S(1)} %bitcast.9, bf16[1,2048,1536]{2,1,0:T(8,128)(2,1)S(1)} %get-tuple-element.29.in_ref, bf16[1,768,2048]{2,1,0:T(8,128)(2,1)S(1)} %copy-done), custom_call_target="tpu_custom_call" | custom-call | tf_op jit(solution)/shard_map/experts/pallas_call | solution.py:269
  47.8 28.8 %all_to_all.11 = bf16[32,8,2048]{2,1,0:T(8,128)(2,1)S(1)} all-to-all(bf16[32,8,2048]{2,1,0:T(8,128)(2,1)S(1)} %bitcast.10), channel_id=1, replica_groups={{0,3,2,1,4,7,6,5,8,11,10,9,12,15,14,13,16,19,18,17,20,23,22,21,24,27,26..., dimensions={0} | all-to-all | bytes 2097152 | tf_op jit(solution)/shard_map/all_to_all | solution.py:343
  76.5 1.0 %combine.1 = bf16[128,2048]{1,0:T(8,128)(2,1)} custom-call(bf16[256,2048]{1,0:T(8,128)(2,1)S(1)} %bitcast.8, bf16[128,2048]{1,0:T(8,128)(2,1)S(1)} %get-tuple-element.30.hidden_ref, bf16[128,256]{1,0:T(8,128)(2,1)S(1)} %get-tuple-element.31.picking_ref, f32[128,128]{1,0:T(8,128)S(1)} %get-tuple-element.32.gates_ref), custom_call_target="tpu_custom_call" | custom-call | tf_op jit(solution)/shard_map/combine/pallas_call | solution.py:299
Async XLA Ops:
  0.0 9.4 %collective-permute-start.3 = (bf16[128,256]{1,0:T(8,128)(2,1)}, bf16[128,256]{1,0:T(8,128)(2,1)S(1)}, u32[]{:S(2)}, u32[]{:S(2)}) collective-permute-start(bf16[128,256]{1,0:T(8,128)(2,1)} %refs_4_.1), channel_id=1, source_target_pairs={{0,1},{1,2},{2,3},{3,0},{4,5},{5,6},{6,7},{7,4},{8,9},{9,10},{10,1... | collective-permute-start | bytes 196616 | tf_op jit(solution)/shard_map/ppermute | solution.py:330
  2.1 7.2 %collective-permute-start.2 = (bf16[128,256]{1,0:T(8,128)(2,1)}, bf16[128,256]{1,0:T(8,128)(2,1)S(1)}, u32[]{:S(2)}, u32[]{:S(2)}) collective-permute-start(bf16[128,256]{1,0:T(8,128)(2,1)} %refs_4_.1), channel_id=1, source_target_pairs={{0,2},{1,3},{2,1},{3,0},{4,6},{5,7},{6,5},{7,4},{8,10},{9,11},{10,... | collective-permute-start | bytes 196616 | tf_op jit(solution)/shard_map/ppermute | solution.py:330
  4.4 6.2 %collective-permute-start = (bf16[128,256]{1,0:T(8,128)(2,1)}, bf16[128,256]{1,0:T(8,128)(2,1)S(1)}, u32[]{:S(2)}, u32[]{:S(2)}) collective-permute-start(bf16[128,256]{1,0:T(8,128)(2,1)} %refs_5_.1), channel_id=1, source_target_pairs={{0,2},{1,3},{2,1},{3,0},{4,6},{5,7},{6,5},{7,4},{8,10},{9,11},{10,... | collective-permute-start | bytes 196616 | tf_op jit(solution)/shard_map/ppermute | solution.py:330
  4.6 6.1 %collective-permute-start.1 = (bf16[128,256]{1,0:T(8,128)(2,1)}, bf16[128,256]{1,0:T(8,128)(2,1)S(1)}, u32[]{:S(2)}, u32[]{:S(2)}) collective-permute-start(bf16[128,256]{1,0:T(8,128)(2,1)} %refs_5_.1), channel_id=1, source_target_pairs={{0,1},{1,2},{2,3},{3,0},{4,5},{5,6},{6,7},{7,4},{8,9},{9,10},{10,1... | collective-permute-start | bytes 196616 | tf_op jit(solution)/shard_map/ppermute | solution.py:330
  5.7 39.5 %copy-start = (bf16[1,768,2048]{2,1,0:T(8,128)(2,1)S(1)}, bf16[1,768,2048]{2,1,0:T(8,128)(2,1)}, u32[]{:S(2)}) copy-start(bf16[1,768,2048]{2,1,0:T(8,128)(2,1)} %down_ref.1) | copy-start | bytes 9437188

commit v6 on v5

--- a/solution.py
+++ b/solution.py
@@ -119,9 +119,13 @@
     )(*[pltpu.with_memory_space_constraint(array, pltpu.HBM) for array in sources])
 
 
-def place_of(device, seq_count):
+def place_of(device, seq_count, exp_count):
     low = device & (seq_count - 1)
-    return device - low + ((seq_count - low) & (seq_count - 1))
+    index = (device - low) // seq_count
+    core, chip = index & 1, index >> 1
+    high, odd = (chip >> 1) & 1, chip & 1
+    index = exp_count - 1 - (((chip >> 2) << 3) | ((high ^ odd) << 2) | (high << 1) | core)
+    return index * seq_count + ((seq_count - low) & (seq_count - 1))
 
 
 def slots_of(ids_row, splits, capacity, axis):
@@ -132,7 +136,10 @@
     rank = jnp.sum(same, axis=1 - axis, keepdims=True).astype(jnp.int32)
     first = (ids_row if axis == 1 else ids_col) * splits
     seq_count = lax.axis_size("seq")
-    return [place_of(first + split, seq_count) * capacity + rank for split in range(splits)]
+    exp_count = lax.axis_size("exp")
+    return [
+        place_of(first + split, seq_count, exp_count) * capacity + rank for split in range(splits)
+    ]
 
 
 def one_hot(slots, slot_at):
@@ -339,6 +346,8 @@
     weights, totals = weigh([*key_blocks, keys], queries, bias)
     hidden, outgoing = mix([*value_blocks, values], weights, totals, resid, gain, placing)
 
+    order = sorted(range(devices), key=lambda device: place_of(device, seq_count, exp_count))
+
     def exchange(block):
         return lax.all_to_all(
             block.reshape(devices, capacity, model_width),
@@ -346,7 +355,7 @@
             split_axis=0,
             concat_axis=0,
             tiled=True,
-            axis_index_groups=[[place_of(device, seq_count) for device in range(devices)]],
+            axis_index_groups=[order],
         ).reshape(slots, model_width)
 
     delivered = exchange(experts(exchange(outgoing), w_in, w_out))

time: 77.8 us -> 77.6 us (level)
  no operation moved by 1% of the time
where the time goes in v6:
time: 77.6 us; the launch traced here: 77 us
  blocking collectives  61.3 us (79%)
  Pallas kernels  9.91 us (13%)
  starting transfers between devices  5.67 us (7%)
    all_to_all x2, blocking collectives, exchange(): lax.all_to_all(block.reshape(devices, capacity, model_width), ('exp', 'se...  61.3 us
    ppermute x4, starting transfers between devices, earlier(): lax.ppermute(own, 'seq', [(i, (i + hop) % seq_count if i + hop < seq_coun...  5.67 us
    pallas_call x1, Pallas kernels, stage(): pl.pallas_call(functools.partial(stage_kernel, before, splits, capacity),...  3.67 us
    pallas_call x1, Pallas kernels, experts(): pl.pallas_call(expert_kernel, out_shape=jax.ShapeDtypeStruct((rows, model...  2.61 us
  transfers between devices with their start and end apart: 4, of which 0 were waited for; matrix products, arithmetic and copies ran while one was open for 0% of the time, Pallas kernels for 6%

profile of v6, /device:TPU:1, one launch (start us, length us, event | category | flops | bytes accessed | tf_op | source)
XLA Modules:
  0.0 77.0 jit_solution(15419923912757484485)
XLA Ops:
  0.0 2.1 %collective-permute-start.3 = (bf16[128,256]{1,0:T(8,128)(2,1)}, bf16[128,256]{1,0:T(8,128)(2,1)S(1)}, u32[]{:S(2)}, u32[]{:S(2)}) collective-permute-start(bf16[128,256]{1,0:T(8,128)(2,1)} %refs_4_.1), channel_id=1, source_target_pairs={{0,1},{1,2},{2,3},{3,0},{4,5},{5,6},{6,7},{7,4},{8,9},{9,10},{10,1... | collective-permute-start | bytes 196616 | tf_op jit(solution)/shard_map/ppermute | solution.py:337
  2.1 2.3 %collective-permute-start.2 = (bf16[128,256]{1,0:T(8,128)(2,1)}, bf16[128,256]{1,0:T(8,128)(2,1)S(1)}, u32[]{:S(2)}, u32[]{:S(2)}) collective-permute-start(bf16[128,256]{1,0:T(8,128)(2,1)} %refs_4_.1), channel_id=1, source_target_pairs={{0,2},{1,3},{2,1},{3,0},{4,6},{5,7},{6,5},{7,4},{8,10},{9,11},{10,... | collective-permute-start | bytes 196616 | tf_op jit(solution)/shard_map/ppermute | solution.py:337
  4.4 0.2 collective-permute-start
  4.6 1.1 %collective-permute-start.1 = (bf16[128,256]{1,0:T(8,128)(2,1)}, bf16[128,256]{1,0:T(8,128)(2,1)S(1)}, u32[]{:S(2)}, u32[]{:S(2)}) collective-permute-start(bf16[128,256]{1,0:T(8,128)(2,1)} %refs_5_.1), channel_id=1, source_target_pairs={{0,1},{1,2},{2,3},{3,0},{4,5},{5,6},{6,7},{7,4},{8,9},{9,10},{10,1... | collective-permute-start | bytes 196616 | tf_op jit(solution)/shard_map/ppermute | solution.py:337
  5.7 0.0 copy-start
  5.7 3.7 %stage.1 = (bf16[128,2048]{1,0:T(8,128)(2,1)S(1)}, bf16[128,256]{1,0:T(8,128)(2,1)S(1)}, bf16[128,256]{1,0:T(8,128)(2,1)S(1)}, bf16[128,2048]{1,0:T(8,128)(2,1)S...) custom-call(s32[1,512]{1,0:T(1,128)} %bitcast.13, ...), custom_call_target="tpu_custom_call" | custom-call | bytes 10485760 | tf_op jit(solution)/shard_map/stage/pallas_call | solution.py:101
  9.4 0.0 collective-permute-done.3.refs_1_
  9.4 0.0 collective-permute-done.2.refs_0_
  9.4 1.3 %weigh.1 = (bf16[8,384,256]{2,1,0:T(8,128)(2,1)S(1)}, f32[8,256]{1,0:T(8,128)S(1)}) custom-call(bf16[128,256]{1,0:T(8,128)(2,1)S(1)} %collective-permute-done.2.refs_0_, bf16[128,256]{1,0:T(8,128)(2,1)S(1)} %collective-permute-done.3.refs_1_, bf16[128,256]{1,0:T(8,128)(2,1)S(1)} %get-tuple-element.20.refs_2_, ...), custom_call_target="tpu_custom_call" | custom-call | flops 402653184 | bytes 1048576 | tf_op jit(solution)/shard_map/weigh/pallas_call | solution.py:176
  10.7 0.0 collective-permute-done.refs_0_
  10.7 0.0 collective-permute-done.1.refs_1_
  10.7 1.3 %mix.1 = (bf16[128,2048]{1,0:T(8,128)(2,1)S(1)}, bf16[256,2048]{1,0:T(8,128)(2,1)S(1)}) custom-call(bf16[128,256]{1,0:T(8,128)(2,1)S(1)} %collective-permute-done.refs_0_, bf16[128,256]{1,0:T(8,128)(2,1)S(1)} %collective-permute-done.1.refs_1_, bf16[128,256]{1,0:T(8,128)(2,1)S(1)} %get-tuple-element.19.refs_2_, ...), custom_call_target="tpu_custom_call" | custom-call | tf_op jit(solution)/shard_map/mix/pallas_call | solution.py:237
  12.0 32.6 %all_to_all.10 = bf16[32,8,2048]{2,1,0:T(8,128)(2,1)S(1)} all-to-all(bf16[32,8,2048]{2,1,0:T(8,128)(2,1)S(1)} %bitcast.11), channel_id=1, replica_groups={{20,23,22,21,16,19,18,17,12,15,14,13,8,11,10,9,28,31,30,29,24,27,26,25,..., dimensions={0} | all-to-all | bytes 2097152 | tf_op jit(solution)/shard_map/all_to_all | solution.py:352
  44.5 0.0 copy-done
  44.5 2.6 %experts.1 = bf16[256,2048]{1,0:T(8,128)(2,1)S(1)} custom-call(bf16[256,2048]{1,0:T(8,128)(2,1)S(1)} %bitcast.9, bf16[1,2048,1536]{2,1,0:T(8,128)(2,1)S(1)} %get-tuple-element.29.in_ref, bf16[1,768,2048]{2,1,0:T(8,128)(2,1)S(1)} %copy-done), custom_call_target="tpu_custom_call" | custom-call | tf_op jit(solution)/shard_map/experts/pallas_call | solution.py:276
  47.2 28.8 %all_to_all.11 = bf16[32,8,2048]{2,1,0:T(8,128)(2,1)S(1)} all-to-all(bf16[32,8,2048]{2,1,0:T(8,128)(2,1)S(1)} %bitcast.10), channel_id=1, replica_groups={{20,23,22,21,16,19,18,17,12,15,14,13,8,11,10,9,28,31,30,29,24,27,26,25,..., dimensions={0} | all-to-all | bytes 2097152 | tf_op jit(solution)/shard_map/all_to_all | solution.py:352
  75.9 1.0 %combine.1 = bf16[128,2048]{1,0:T(8,128)(2,1)} custom-call(bf16[256,2048]{1,0:T(8,128)(2,1)S(1)} %bitcast.8, bf16[128,2048]{1,0:T(8,128)(2,1)S(1)} %get-tuple-element.30.hidden_ref, bf16[128,256]{1,0:T(8,128)(2,1)S(1)} %get-tuple-element.31.picking_ref, f32[128,128]{1,0:T(8,128)S(1)} %get-tuple-element.32.gates_ref), custom_call_target="tpu_custom_call" | custom-call | tf_op jit(solution)/shard_map/combine/pallas_call | solution.py:306
Async XLA Ops:
  0.0 9.4 %collective-permute-start.3 = (bf16[128,256]{1,0:T(8,128)(2,1)}, bf16[128,256]{1,0:T(8,128)(2,1)S(1)}, u32[]{:S(2)}, u32[]{:S(2)}) collective-permute-start(bf16[128,256]{1,0:T(8,128)(2,1)} %refs_4_.1), channel_id=1, source_target_pairs={{0,1},{1,2},{2,3},{3,0},{4,5},{5,6},{6,7},{7,4},{8,9},{9,10},{10,1... | collective-permute-start | bytes 196616 | tf_op jit(solution)/shard_map/ppermute | solution.py:337
  2.1 7.2 %collective-permute-start.2 = (bf16[128,256]{1,0:T(8,128)(2,1)}, bf16[128,256]{1,0:T(8,128)(2,1)S(1)}, u32[]{:S(2)}, u32[]{:S(2)}) collective-permute-start(bf16[128,256]{1,0:T(8,128)(2,1)} %refs_4_.1), channel_id=1, source_target_pairs={{0,2},{1,3},{2,1},{3,0},{4,6},{5,7},{6,5},{7,4},{8,10},{9,11},{10,... | collective-permute-start | bytes 196616 | tf_op jit(solution)/shard_map/ppermute | solution.py:337
  4.4 6.2 %collective-permute-start = (bf16[128,256]{1,0:T(8,128)(2,1)}, bf16[128,256]{1,0:T(8,128)(2,1)S(1)}, u32[]{:S(2)}, u32[]{:S(2)}) collective-permute-start(bf16[128,256]{1,0:T(8,128)(2,1)} %refs_5_.1), channel_id=1, source_target_pairs={{0,2},{1,3},{2,1},{3,0},{4,6},{5,7},{6,5},{7,4},{8,10},{9,11},{10,... | collective-permute-start | bytes 196616 | tf_op jit(solution)/shard_map/ppermute | solution.py:337
  4.6 6.1 %collective-permute-start.1 = (bf16[128,256]{1,0:T(8,128)(2,1)}, bf16[128,256]{1,0:T(8,128)(2,1)S(1)}, u32[]{:S(2)}, u32[]{:S(2)}) collective-permute-start(bf16[128,256]{1,0:T(8,128)(2,1)} %refs_5_.1), channel_id=1, source_target_pairs={{0,1},{1,2},{2,3},{3,0},{4,5},{5,6},{6,7},{7,4},{8,9},{9,10},{10,1... | collective-permute-start | bytes 196616 | tf_op jit(solution)/shard_map/ppermute | solution.py:337
  5.7 38.9 %copy-start = (bf16[1,768,2048]{2,1,0:T(8,128)(2,1)S(1)}, bf16[1,768,2048]{2,1,0:T(8,128)(2,1)}, u32[]{:S(2)}) copy-start(bf16[1,768,2048]{2,1,0:T(8,128)(2,1)} %down_ref.1) | copy-start | bytes 9437188
